TPU v7x, 32 devices: a whole 2x2x4 slice. The times are simulated.
32 devices in a mesh: box: 8 (over z, core), dir: 4 (over y, x).
Axes of the slice: x: 2, y: 2, z: 4, core: 2. Of those that a mesh axis runs over, the one named last changes fastest.
Arguments:
- currents: float32 [4096, 2, 128], P(('box', 'dir')), may hold values from -6 to 6
- near_blocks: float32 [16, 2, 128, 128], replicated, may hold values from -0.078125 to 0.078125
- block_ids: int32 [4096, 27], P(('box', 'dir')), may hold values from 0 to 15
- neighbors: int32 [4096, 27], P(('box', 'dir')), may hold values from 0 to 4095, as said below
- leaf_place: int32 [4096, 2], P(('box', 'dir')), may hold values from 0 to 255, as said below
- radiation: float32 [2, 128, 128], replicated, may hold values from -0.375 to 0.375
- interpolation: float32 [128, 8192], replicated, may hold values from -0.5 to 0.5
- translation: float32 [8192, 2, 316], P('dir'), may hold values from -0.625 to 0.625
- list_src: int32 [256, 40], replicated, may hold values from 0 to 255, as said below
- list_offset: int32 [256, 40], replicated, may hold values from 0 to 315
Outputs:
- product: float32 [4096, 2, 128], P(('box', 'dir'))
Inputs may be any that keep to these rules, and one draw needn't show every extreme that they name: `neighbors`: the neighbours of a leaf stored on device i (devices numbered over box, then dir) are stored on device i - 1, i or i + 1. `leaf_place`: the parent of a leaf stored on a device of box index b is one of the 32 coarse boxes b * 32 to (b + 1) * 32 - 1 owned by b; the position code lies in 0 to 63. `list_src`: coarse box c belongs to box index c // 32; for every pair of box indices b, p the lists of b's coarse boxes name exactly 8 distinct coarse boxes of p.
All inputs are finite; a program needn't handle non-finite values.
Results may differ from a plain program's by a relative error of at most 0.0003.
Values sent between devices are 32-bit elements; how exact they have to be, the bound alone decides.
A program may use at most 128 MiB of HBM per device.

v0:
```python
import math

import jax
import jax.numpy as jnp
from jax import lax
from jax.sharding import PartitionSpec as P

kappa_leaf = math.pi
highest = lax.Precision.HIGHEST


def padded(block, sides, width):
    for axis, dim in sides:
        count = lax.axis_size(axis)
        forward = [(i, i + 1) for i in range(count - 1)]
        backward = [(target, source) for source, target in forward]
        low = lax.ppermute(
            lax.slice_in_dim(block, block.shape[dim] - width, None, axis=dim), axis, forward
        )
        high = lax.ppermute(lax.slice_in_dim(block, 0, width, axis=dim), axis, backward)
        block = jnp.concatenate([low, block, high], axis=dim)
    return block


def matmul(left, right):
    return jnp.dot(left, right, precision=highest, preferred_element_type=jnp.float32)


def phases(position, count, polar):
    order = jnp.arange(count, dtype=jnp.int32)
    cycle = order // (2 * polar)
    beside_all = order % (2 * polar)
    theta = math.pi * (cycle.astype(jnp.float32) + 0.5) / polar
    azimuth = math.pi * beside_all.astype(jnp.float32) / polar
    along_x = jnp.sin(theta) * jnp.cos(azimuth)
    along_y = jnp.sin(theta) * jnp.sin(azimuth)
    along_z = jnp.cos(theta)
    off_x = (position % 4).astype(jnp.float32) - 1.5
    off_y = (position // 4 % 4).astype(jnp.float32) - 1.5
    off_z = (position // 16).astype(jnp.float32) - 1.5
    angle = kappa_leaf * (
        off_x[:, None] * along_x[None, :]
        + off_y[:, None] * along_y[None, :]
        + off_z[:, None] * along_z[None, :]
    )
    return (jnp.cos(angle), jnp.sin(angle), jnp.sin(theta))


def near_field(gathered, local, kinds, near_blocks):
    rows = jnp.take(gathered, local, axis=0)
    count = near_blocks.shape[0]
    onehot = (kinds[..., None] == jnp.arange(count, dtype=jnp.int32)).astype(jnp.float32)
    summed = jnp.einsum("ljt,ljrn->trln", onehot, rows, precision=highest)
    block_r = near_blocks[:, 0]
    block_i = near_blocks[:, 1]
    real = jnp.einsum("tmn,tln->lm", block_r, summed[:, 0], precision=highest) - jnp.einsum(
        "tmn,tln->lm", block_i, summed[:, 1], precision=highest
    )
    imag = jnp.einsum("tmn,tln->lm", block_r, summed[:, 1], precision=highest) + jnp.einsum(
        "tmn,tln->lm", block_i, summed[:, 0], precision=highest
    )
    return jnp.stack([real, imag], 1)


def radiate(cur, radiation):
    real = matmul(cur[:, 0], radiation[0]) - matmul(cur[:, 1], radiation[1])
    imag = matmul(cur[:, 0], radiation[1]) + matmul(cur[:, 1], radiation[0])
    return (real, imag)


def receive(real, imag, radiation):
    out_r = matmul(real, radiation[0].T) + matmul(imag, radiation[1].T)
    out_i = matmul(imag, radiation[0].T) - matmul(real, radiation[1].T)
    return jnp.stack([out_r, out_i], 1)


def parent_table(parents, box_base, boxes):
    return ((parents - box_base)[None, :] == jnp.arange(boxes, dtype=jnp.int32)[:, None]).astype(
        jnp.float32
    )


def translate(source, index, offsets, translation):
    k1_dev = translation.shape[0]
    boxes = index.shape[0]

    def block(step, acc):
        ids = lax.dynamic_slice_in_dim(index, step * 8, 8, 1).reshape(-1)
        offs = lax.dynamic_slice_in_dim(offsets, step * 8, 8, 1).reshape(-1)
        picked = jnp.take(source, ids, axis=2)
        table = jnp.take(translation, offs, axis=2)
        real = table[:, 0] * picked[:, 0] - table[:, 1] * picked[:, 1]
        imag = table[:, 0] * picked[:, 1] + table[:, 1] * picked[:, 0]
        both = jnp.stack([real, imag], 1).reshape(k1_dev, 2, boxes, 8)
        return acc + jnp.sum(both, axis=3)

    return lax.fori_loop(0, index.shape[1] // 8, block, jnp.zeros((k1_dev, 2, boxes), jnp.float32))


def on_device(
    currents,
    near_blocks,
    block_ids,
    neighbors,
    leaf_place,
    radiation,
    interpolation,
    translation,
    list_src,
    list_offset,
):
    leaf_count = currents.shape[0]
    count_k0 = interpolation.shape[0]
    count_k1 = interpolation.shape[1]
    polar = math.isqrt(count_k1 // 2)
    scale = math.sqrt(count_k0 / count_k1)
    k1_dev = translation.shape[0]
    nboxes = lax.axis_size("box")
    boxes = list_src.shape[0] // nboxes
    box_base = lax.axis_index("box") * boxes
    gathered = padded(currents, ((("box", "dir"), 0),), leaf_count)
    local = neighbors - (lax.axis_index(("box", "dir")) - 1) * leaf_count
    near = near_field(gathered, local, block_ids, near_blocks)
    s0_r, s0_i = radiate(currents, radiation)
    parent_hot = parent_table(leaf_place[:, 0], box_base, boxes)
    position = leaf_place[:, 1]
    part = interpolation
    wave_r = matmul(s0_r, part)
    wave_i = matmul(s0_i, part)
    cosine, sine, unused = phases(position, k1_dev * lax.axis_size("dir"), polar)
    shift_r = wave_r * cosine + wave_i * sine
    shift_i = wave_i * cosine - wave_r * sine
    sum_r = jnp.einsum("cl,lk->kc", parent_hot, shift_r, precision=highest)
    sum_i = jnp.einsum("cl,lk->kc", parent_hot, shift_i, precision=highest)
    coarse = lax.psum_scatter(jnp.stack([sum_r, sum_i], 1), "dir", scatter_dimension=0, tiled=True)
    mine_src = lax.dynamic_slice_in_dim(list_src, box_base, boxes, 0)
    mine_off = lax.dynamic_slice_in_dim(list_offset, box_base, boxes, 0)
    everything = lax.all_gather(coarse, "box", axis=2, tiled=True)
    fields = translate(everything, mine_src, mine_off, translation)
    piece = lax.all_gather(fields, "dir", axis=0, tiled=True)
    count = piece.shape[0]
    part = interpolation
    field_r = jnp.einsum("cl,kc->lk", parent_hot, piece[:, 0], precision=highest)
    field_i = jnp.einsum("cl,kc->lk", parent_hot, piece[:, 1], precision=highest)
    cosine, sine, polar_sine = phases(position, count, polar)
    weight = polar_sine * scale
    back_r = (field_r * cosine - field_i * sine) * weight
    back_i = (field_r * sine + field_i * cosine) * weight
    far_r = matmul(back_r, part.T)
    far_i = matmul(back_i, part.T)
    return near + receive(far_r, far_i, radiation)


def solution(mesh):
    placed = (
        P(("box", "dir"), None, None),
        P(),
        P(("box", "dir"), None),
        P(("box", "dir"), None),
        P(("box", "dir"), None),
        P(),
        P(),
        P("dir", None, None),
        P(),
        P(),
    )
    return jax.shard_map(
        on_device,
        mesh=mesh,
        in_specs=placed,
        out_specs=P(("box", "dir"), None, None),
        check_vma=False,
    )
```

profile of v0, /device:TPU:27, one launch (start us, length us, event | category | flops | bytes accessed | tf_op | source)
XLA Modules:
  0.0 483.7 jit_solution(6465595370886206952)
XLA Ops:
  13.6 5.8 %fusion.139 = f32[128,8192]{1,0:T(8,128)S(1)} fusion(f32[128,128]{1,0:T(8,128)S(1)} %convolution_subtract_fusion.1, f32[128,8192]{1,0:T(8,128)} %param.18), kind=kOutput, calls=%fused_computation.195 | convolution fusion | flops 1610612736 | bytes 8454144 | tf_op jit(solution)/shard_map/dot_general | solution.py:26
  23.5 17.9 %convolution_bitcast_fusion = f32[8192,1,32]{0,2,1:T(8,128)S(1)} fusion(f32[128,8192]{1,0:T(8,128)S(1)} %fusion.139, f32[128,8192]{1,0:T(8,128)S(1)} %fusion.140, f32[8192]{0:T(1024)S(1)} %fusion.119, f32[128]{0:T(128)S(1)} %get-tuple-element.179, f32[8192]{0:T(1024)S(1)} %get-tuple-element.183, f32[128]{0:T(128)S(1)} %get-tuple-element.178, ...), kind=kOutput, calls=%fused_computation.21 | convolution fusion | flops 412094464 | bytes 9537536 | tf_op jit(solution)/shard_map/cl,lk->kc/dot_general | solution.py:134
  41.4 18.1 %convolution_bitcast_fusion.1 = f32[8192,1,32]{0,2,1:T(8,128)S(1)} fusion(f32[128,8192]{1,0:T(8,128)S(1)} %fusion.140, f32[128,8192]{1,0:T(8,128)S(1)} %fusion.139, f32[8192]{0:T(1024)S(1)} %fusion.119, f32[128]{0:T(128)S(1)} %get-tuple-element.179, f32[8192]{0:T(1024)S(1)} %get-tuple-element.183, f32[128]{0:T(128)S(1)} %get-tuple-element.178, ...), kind=kOutput, calls=%fused_computation.22 | convolution fusion | flops 412094464 | bytes 9537536 | tf_op jit(solution)/shard_map/cl,lk->kc/dot_general | solution.py:133
  61.1 36.2 %reduce-scatter.2.cloned.1.call-done = f32[2048,2,32]{0,2,1:T(8,128)} async-done(((f32[8192,2,32]{0,2,1:T(8,128)}), f32[2048,2,32]{0,2,1:T(8,128)}) %reduce-scatter.2.cloned.1.call-update) | async-done | bytes 524304 | tf_op jit(solution)/shard_map/reduce_scatter | solution.py:135
  97.5 47.0 %all-gather.3.cloned.1.call-done = f32[2048,2,256]{0,2,1:T(8,128)} async-done(((f32[2048,2,32]{0,2,1:T(8,128)}), f32[2048,2,256]{0,2,1:T(8,128)}) %all-gather.3.cloned.1.call-update) | async-done | bytes 4194320 | tf_op jit(solution)/shard_map/all_gather | solution.py:138
  144.4 7.4 %copy.50 = f32[2048,2,256]{0,1,2:T(2,128)} copy(f32[2048,2,256]{0,2,1:T(8,128)} %all-gather.3.cloned.1.call-done) | data formatting | bytes 8388608
  151.8 231.6 %while.14 = (s32[]{:T(128)}, f32[2048,2,32]{0,2,1:T(8,128)S(1)}, s32[32,40]{0,1:T(8,128)S(1)}, f32[2048,2,316]{0,1,2:T(2,128)}, s32[32,40]{0,1:T(8,128)S(1)}, /*...) while((s32[]{:T(128)}, f32[2048,2,32]{0,2,1:T(8,128)S(1)}, ...), condition=%wide.region_3.4_spmd.clone, body=%wide.region_1.3_spmd.clone.sunk | while | flops 7477767 | bytes 77630656 | solution.py:97
  152.2 13.5 %gather_fusion.1 = f32[256,2048,2]{1,2,0:T(2,128)} fusion(f32[2048,2,316]{0,1,2:T(2,128)} %get-tuple-element.252, s32[1024]{0:T(1024)S(1)} %pad_clamp_fusion.6), kind=kCustom, calls=%fused_computation.clone.clone.1 | custom fusion | bytes 8389632 | tf_op jit(solution)/shard_map/while/body/eval_jaxpr/jit(_take)/gather | solution.py:91
  165.7 6.1 %select_bitcast_fusion.5 = f32[2048,2,256]{0,1,2:T(2,128)} fusion(f32[256,2048,2]{1,2,0:T(2,128)} %gather_fusion.1, pred[256]{0:T(512)(128)(4,1)S(1)} %compare_and_fusion.6), kind=kLoop, calls=%fused_computation.5.clone.1 | loop fusion | flops 1048576 | bytes 8388864 | tf_op jit(solution)/shard_map/while/body/eval_jaxpr/jit(_take)/select_n | solution.py:91
  172.0 13.2 %gather_fusion = f32[256,2048,2]{1,2,0:T(2,128)} fusion(f32[2048,2,256]{0,1,2:T(2,128)} %get-tuple-element.254, s32[1024]{0:T(1024)S(1)} %pad_clamp_fusion.5), kind=kCustom, calls=%fused_computation.1.clone.clone.1 | custom fusion | bytes 8389632 | tf_op jit(solution)/shard_map/while/body/eval_jaxpr/jit(_take)/gather | solution.py:90
  189.6 5.6 %multiply_subtract_fusion.2 = (f32[2048,1,256]{0,1,2:T(1,128)S(1)}, f32[2048,1,256]{0,1,2:T(1,128)S(1)}) fusion(f32[2048,2,256]{0,1,2:T(2,128)S(1)} %select_bitcast_fusion.4, f32[2048,2,256]{0,1,2:T(2,128)S(1)} %copy-done), kind=kLoop, calls=%fused_computation.9.clone.1 | loop fusion | flops 3145728 | bytes 12582912 | tf_op jit(solution)/shard_map/while/body/eval_jaxpr/sub | solution.py:92
  198.4 13.5 %gather_fusion.1 = f32[256,2048,2]{1,2,0:T(2,128)} fusion(f32[2048,2,316]{0,1,2:T(2,128)} %get-tuple-element.252, s32[1024]{0:T(1024)S(1)} %pad_clamp_fusion.6), kind=kCustom, calls=%fused_computation.clone.clone.1 | custom fusion | bytes 8389632 | tf_op jit(solution)/shard_map/while/body/eval_jaxpr/jit(_take)/gather | solution.py:91
  211.9 6.1 %select_bitcast_fusion.5 = f32[2048,2,256]{0,1,2:T(2,128)} fusion(f32[256,2048,2]{1,2,0:T(2,128)} %gather_fusion.1, pred[256]{0:T(512)(128)(4,1)S(1)} %compare_and_fusion.6), kind=kLoop, calls=%fused_computation.5.clone.1 | loop fusion | flops 1048576 | bytes 8388864 | tf_op jit(solution)/shard_map/while/body/eval_jaxpr/jit(_take)/select_n | solution.py:91
  218.2 13.2 %gather_fusion = f32[256,2048,2]{1,2,0:T(2,128)} fusion(f32[2048,2,256]{0,1,2:T(2,128)} %get-tuple-element.254, s32[1024]{0:T(1024)S(1)} %pad_clamp_fusion.5), kind=kCustom, calls=%fused_computation.1.clone.clone.1 | custom fusion | bytes 8389632 | tf_op jit(solution)/shard_map/while/body/eval_jaxpr/jit(_take)/gather | solution.py:90
  235.8 5.6 %multiply_subtract_fusion.2 = (f32[2048,1,256]{0,1,2:T(1,128)S(1)}, f32[2048,1,256]{0,1,2:T(1,128)S(1)}) fusion(f32[2048,2,256]{0,1,2:T(2,128)S(1)} %select_bitcast_fusion.4, f32[2048,2,256]{0,1,2:T(2,128)S(1)} %copy-done), kind=kLoop, calls=%fused_computation.9.clone.1 | loop fusion | flops 3145728 | bytes 12582912 | tf_op jit(solution)/shard_map/while/body/eval_jaxpr/sub | solution.py:92
  244.6 13.5 %gather_fusion.1 = f32[256,2048,2]{1,2,0:T(2,128)} fusion(f32[2048,2,316]{0,1,2:T(2,128)} %get-tuple-element.252, s32[1024]{0:T(1024)S(1)} %pad_clamp_fusion.6), kind=kCustom, calls=%fused_computation.clone.clone.1 | custom fusion | bytes 8389632 | tf_op jit(solution)/shard_map/while/body/eval_jaxpr/jit(_take)/gather | solution.py:91
  258.1 6.1 %select_bitcast_fusion.5 = f32[2048,2,256]{0,1,2:T(2,128)} fusion(f32[256,2048,2]{1,2,0:T(2,128)} %gather_fusion.1, pred[256]{0:T(512)(128)(4,1)S(1)} %compare_and_fusion.6), kind=kLoop, calls=%fused_computation.5.clone.1 | loop fusion | flops 1048576 | bytes 8388864 | tf_op jit(solution)/shard_map/while/body/eval_jaxpr/jit(_take)/select_n | solution.py:91
  264.4 13.2 %gather_fusion = f32[256,2048,2]{1,2,0:T(2,128)} fusion(f32[2048,2,256]{0,1,2:T(2,128)} %get-tuple-element.254, s32[1024]{0:T(1024)S(1)} %pad_clamp_fusion.5), kind=kCustom, calls=%fused_computation.1.clone.clone.1 | custom fusion | bytes 8389632 | tf_op jit(solution)/shard_map/while/body/eval_jaxpr/jit(_take)/gather | solution.py:90
  282.0 5.6 %multiply_subtract_fusion.2 = (f32[2048,1,256]{0,1,2:T(1,128)S(1)}, f32[2048,1,256]{0,1,2:T(1,128)S(1)}) fusion(f32[2048,2,256]{0,1,2:T(2,128)S(1)} %select_bitcast_fusion.4, f32[2048,2,256]{0,1,2:T(2,128)S(1)} %copy-done), kind=kLoop, calls=%fused_computation.9.clone.1 | loop fusion | flops 3145728 | bytes 12582912 | tf_op jit(solution)/shard_map/while/body/eval_jaxpr/sub | solution.py:92
  290.8 13.5 %gather_fusion.1 = f32[256,2048,2]{1,2,0:T(2,128)} fusion(f32[2048,2,316]{0,1,2:T(2,128)} %get-tuple-element.252, s32[1024]{0:T(1024)S(1)} %pad_clamp_fusion.6), kind=kCustom, calls=%fused_computation.clone.clone.1 | custom fusion | bytes 8389632 | tf_op jit(solution)/shard_map/while/body/eval_jaxpr/jit(_take)/gather | solution.py:91
  304.3 6.1 %select_bitcast_fusion.5 = f32[2048,2,256]{0,1,2:T(2,128)} fusion(f32[256,2048,2]{1,2,0:T(2,128)} %gather_fusion.1, pred[256]{0:T(512)(128)(4,1)S(1)} %compare_and_fusion.6), kind=kLoop, calls=%fused_computation.5.clone.1 | loop fusion | flops 1048576 | bytes 8388864 | tf_op jit(solution)/shard_map/while/body/eval_jaxpr/jit(_take)/select_n | solution.py:91
  310.6 13.2 %gather_fusion = f32[256,2048,2]{1,2,0:T(2,128)} fusion(f32[2048,2,256]{0,1,2:T(2,128)} %get-tuple-element.254, s32[1024]{0:T(1024)S(1)} %pad_clamp_fusion.5), kind=kCustom, calls=%fused_computation.1.clone.clone.1 | custom fusion | bytes 8389632 | tf_op jit(solution)/shard_map/while/body/eval_jaxpr/jit(_take)/gather | solution.py:90
  328.2 5.6 %multiply_subtract_fusion.2 = (f32[2048,1,256]{0,1,2:T(1,128)S(1)}, f32[2048,1,256]{0,1,2:T(1,128)S(1)}) fusion(f32[2048,2,256]{0,1,2:T(2,128)S(1)} %select_bitcast_fusion.4, f32[2048,2,256]{0,1,2:T(2,128)S(1)} %copy-done), kind=kLoop, calls=%fused_computation.9.clone.1 | loop fusion | flops 3145728 | bytes 12582912 | tf_op jit(solution)/shard_map/while/body/eval_jaxpr/sub | solution.py:92
  337.0 13.5 %gather_fusion.1 = f32[256,2048,2]{1,2,0:T(2,128)} fusion(f32[2048,2,316]{0,1,2:T(2,128)} %get-tuple-element.252, s32[1024]{0:T(1024)S(1)} %pad_clamp_fusion.6), kind=kCustom, calls=%fused_computation.clone.clone.1 | custom fusion | bytes 8389632 | tf_op jit(solution)/shard_map/while/body/eval_jaxpr/jit(_take)/gather | solution.py:91
  350.6 6.1 %select_bitcast_fusion.5 = f32[2048,2,256]{0,1,2:T(2,128)} fusion(f32[256,2048,2]{1,2,0:T(2,128)} %gather_fusion.1, pred[256]{0:T(512)(128)(4,1)S(1)} %compare_and_fusion.6), kind=kLoop, calls=%fused_computation.5.clone.1 | loop fusion | flops 1048576 | bytes 8388864 | tf_op jit(solution)/shard_map/while/body/eval_jaxpr/jit(_take)/select_n | solution.py:91
  356.8 13.2 %gather_fusion = f32[256,2048,2]{1,2,0:T(2,128)} fusion(f32[2048,2,256]{0,1,2:T(2,128)} %get-tuple-element.254, s32[1024]{0:T(1024)S(1)} %pad_clamp_fusion.5), kind=kCustom, calls=%fused_computation.1.clone.clone.1 | custom fusion | bytes 8389632 | tf_op jit(solution)/shard_map/while/body/eval_jaxpr/jit(_take)/gather | solution.py:90
  374.4 5.6 %multiply_subtract_fusion.2 = (f32[2048,1,256]{0,1,2:T(1,128)S(1)}, f32[2048,1,256]{0,1,2:T(1,128)S(1)}) fusion(f32[2048,2,256]{0,1,2:T(2,128)S(1)} %select_bitcast_fusion.4, f32[2048,2,256]{0,1,2:T(2,128)S(1)} %copy-done), kind=kLoop, calls=%fused_computation.9.clone.1 | loop fusion | flops 3145728 | bytes 12582912 | tf_op jit(solution)/shard_map/while/body/eval_jaxpr/sub | solution.py:92
  394.8 10.5 %gather_fusion.2 = f32[3456,2,128]{2,1,0:T(2,128)} fusion(f32[384,2,128]{2,1,0:T(2,128)S(1)} %pad_maximum_fusion.1, s32[4096]{0:T(1024)S(1)} %pad_clamp_fusion.2), kind=kCustom, calls=%fused_computation.2 | custom fusion | bytes 7091712 | tf_op jit(solution)/shard_map/jit(_take)/gather | solution.py:50
  405.3 4.8 fusion.59
  415.2 5.3 %all-gather.5.cloned.1.call-done = f32[8192,2,32]{0,2,1:T(8,128)} async-done(((f32[2048,2,32]{0,2,1:T(8,128)}), f32[8192,2,32]{0,2,1:T(8,128)}) %all-gather.5.cloned.1.call-update) | async-done | bytes 2097168 | tf_op jit(solution)/shard_map/all_gather | solution.py:140
  426.8 24.1 %fusion.6 = f32[128,128]{1,0:T(8,128)S(1)} fusion(f32[128,8192]{1,0:T(8,128)S(1)} %copy-done.3, f32[128,8192]{1,0:T(8,128)S(1)} %fusion.66, f32[128,8192]{1,0:T(8,128)S(1)} %fusion.67, f32[8192]{0:T(1024)S(1)} %fusion.121, f32[8192]{0:T(1024)S(1)} %fusion.119, f32[128]{0:T(128)S(1)} %get-tuple-element.179, f32[8192]{0:T(1024)S(1)} %get-tuple-element.183, ...), kind=kOutput, calls=%fused_computation.30 | convolution fusion | flops 1621098496 | bytes 12781056 | tf_op jit(solution)/shard_map/dot_general | solution.py:26
  450.9 24.1 %fusion.1 = f32[128,128]{1,0:T(8,128)S(1)} fusion(f32[128,8192]{1,0:T(8,128)S(1)} %copy-done.3, f32[128,8192]{1,0:T(8,128)S(1)} %fusion.66, f32[128,8192]{1,0:T(8,128)S(1)} %fusion.67, f32[8192]{0:T(1024)S(1)} %fusion.121, f32[8192]{0:T(1024)S(1)} %fusion.119, f32[128]{0:T(128)S(1)} %get-tuple-element.179, f32[8192]{0:T(1024)S(1)} %get-tuple-element.183, ...), kind=kOutput, calls=%fused_computation.25 | convolution fusion | flops 1621098496 | bytes 12781056 | tf_op jit(solution)/shard_map/dot_general | solution.py:26
  (167 shorter events, 75.8 us)
Async XLA Ops:
  6.5 90.7 %reduce-scatter.2.cloned.1.call-start = ((), (), s32[]{:S(2)}) async-start(), calls=%async_computation.1 | async-start | bytes 2621440 | tf_op jit(solution)/shard_map/reduce_scatter | solution.py:135
  13.6 5.8 %copy-start.2 = (f32[128,8192]{1,0:T(8,128)S(1)}, f32[128,8192]{1,0:T(8,128)}, u32[]{:S(2)}) copy-start(f32[128,8192]{1,0:T(8,128)} %param.18) | copy-start | bytes 12582916
  19.4 4.0 copy-start.11
  59.5 37.8 %copy-start.9 = (s32[256,40]{0,1:T(8,128)S(1)}, s32[256,40]{0,1:T(8,128)}, u32[]{:S(2)}) copy-start(s32[256,40]{0,1:T(8,128)} %param.20) | copy-start | bytes 122884
  59.5 37.8 %copy-start.10 = (s32[256,40]{0,1:T(8,128)S(1)}, s32[256,40]{0,1:T(8,128)}, u32[]{:S(2)}) copy-start(s32[256,40]{0,1:T(8,128)} %param.21) | copy-start | bytes 122884
  61.0 83.4 %all-gather.3.cloned.1.call-start = ((), (), s32[]{:S(2)}) async-start(), calls=%async_computation.2 | async-start | bytes 4718592 | tf_op jit(solution)/shard_map/all_gather | solution.py:138
  97.3 323.2 %all-gather.5.cloned.1.call-start = ((), (), s32[]{:S(2)}) async-start(), calls=%async_computation.3 | async-start | bytes 2621440 | tf_op jit(solution)/shard_map/all_gather | solution.py:140
  151.8 232.5 %copy-start.6 = (f32[128,2,128]{2,1,0:T(2,128)S(1)}, f32[128,2,128]{2,1,0:T(2,128)}, u32[]{:S(2)}) copy-start(f32[128,2,128]{2,1,0:T(2,128)} %param.12) | copy-start | bytes 393220
  151.8 237.8 %copy-start.8 = (s32[128,27]{0,1:T(8,128)S(1)}, s32[128,27]{0,1:T(8,128)}, u32[]{:S(2)}) copy-start(s32[128,27]{0,1:T(8,128)} %param.15) | copy-start | bytes 41476
  151.8 238.3 %copy-start.7 = (s32[128,27]{0,1:T(8,128)S(1)}, s32[128,27]{0,1:T(8,128)}, u32[]{:S(2)}) copy-start(s32[128,27]{0,1:T(8,128)} %param.14) | copy-start | bytes 41476
  185.3 4.3 copy-start
  231.5 4.3 copy-start
  277.7 4.3 copy-start
  323.9 4.3 copy-start
  370.2 4.3 copy-start
  383.4 0.8 copy-start.1
  384.2 6.7 %collective-permute-start = (f32[128,2,128]{2,1,0:T(2,128)S(1)}, f32[128,2,128]{2,1,0:T(2,128)S(1)}, u32[]{:S(2)}, u32[]{:S(2)}) collective-permute-start(f32[128,2,128]{2,1,0:T(2,128)S(1)} %copy-done.6), channel_id=1, source_target_pairs={{0,1},{1,2},{2,3},{3,4},{4,5},{5,6},{6,7},{7,8},{8,9},{9,10},{10,1... | collective-permute-start | bytes 393224 | tf_op jit(solution)/shard_map/ppermute | solution.py:17
  387.3 7.3 %collective-permute-start.1 = (f32[128,2,128]{2,1,0:T(2,128)S(1)}, f32[128,2,128]{2,1,0:T(2,128)S(1)}, u32[]{:S(2)}, u32[]{:S(2)}) collective-permute-start(f32[128,2,128]{2,1,0:T(2,128)S(1)} %copy-done.6), channel_id=1, source_target_pairs={{1,0},{2,1},{3,2},{4,3},{5,4},{6,5},{7,6},{8,7},{9,8},{10,9},{11,1... | collective-permute-start | bytes 393224 | tf_op jit(solution)/shard_map/ppermute | solution.py:20
  405.3 5.0 %copy-start.4 = (f32[16,2,128,128]{3,2,1,0:T(8,128)S(1)}, f32[16,2,128,128]{3,2,1,0:T(8,128)}, u32[]{:S(2)}) copy-start(f32[16,2,128,128]{3,2,1,0:T(8,128)} %param.13) | copy-start | bytes 6291460
  420.5 6.3 %copy-start.3 = (f32[128,8192]{1,0:T(8,128)S(1)}, f32[128,8192]{1,0:T(8,128)}, u32[]{:S(2)}) copy-start(f32[128,8192]{1,0:T(8,128)} %param.18) | copy-start | bytes 12582916
  450.9 24.1 %copy-start.5 = (f32[2,128,128]{2,1,0:T(8,128)S(1)}, f32[2,128,128]{2,1,0:T(8,128)}, u32[]{:S(2)}) copy-start(f32[2,128,128]{2,1,0:T(8,128)} %param.17) | copy-start | bytes 393220
Sparse Core Ops, SparseCore 0:
  61.1 36.0 reduce-scatter.1
  99.0 45.4 all-gather.2
  384.4 36.1 all-gather.4
where the time goes:
time: 489 us; the launch traced here: 484 us
  local copies, waits for them, and re-layouts  166 us (34%)
  matrix products  115 us (24%)
  waiting for transfers between devices  92.9 us (19%)
  other arithmetic  89.2 us (18%)
  between operations  13.7 us (3%)
  starting transfers between devices  5.36 us (1%)
    gather x5, local copies, waits for them, and re-layouts, block(): table = jnp.take(translation, offs, axis=2)  67.3 us
    gather x5, local copies, waits for them, and re-layouts, block(): picked = jnp.take(source, ids, axis=2)  66.2 us
    dot_general x12, matrix products, matmul(): jnp.dot(left, right, precision=highest, preferred_element_type=jnp.float32)  63.2 us
    all_gather x1, waiting for transfers between devices, on_device(): everything = lax.all_gather(coarse, 'box', axis=2, tiled=True)  47 us
    reduce_scatter x1, waiting for transfers between devices, on_device(): lax.psum_scatter(jnp.stack([sum_r, sum_i], 1), 'dir', scatter_dimension=0...  36.2 us
    select_n x10, other arithmetic, block(): table = jnp.take(translation, offs, axis=2)  30.4 us
    sub x5, other arithmetic, block(): real = table[:, 0] * picked[:, 0] - table[:, 1] * picked[:, 1]  28.1 us
    select_n x10, other arithmetic, block(): picked = jnp.take(source, ids, axis=2)  21.2 us
  transfers between devices with their start and end apart: 5, of which 5 were waited for; matrix products, arithmetic and copies ran while one was open for 4% of the time, Pallas kernels for 0%

commit v1 on v0

v1 whole, which is shorter than its diff:
```python
import functools
import math

import jax
import jax.numpy as jnp
from jax import lax
from jax.experimental import pallas as pl
from jax.experimental.pallas import tpu as pltpu
from jax.sharding import PartitionSpec as P

kappa_leaf = math.pi
high = lax.Precision.HIGH
need = 8
MESH = pl.DeviceIdType.MESH


def padded(block, sides, width):
    for axis, dim in sides:
        count = lax.axis_size(axis)
        forward = [(i, i + 1) for i in range(count - 1)]
        backward = [(target, source) for source, target in forward]
        low = lax.ppermute(
            lax.slice_in_dim(block, block.shape[dim] - width, None, axis=dim), axis, forward
        )
        high_side = lax.ppermute(lax.slice_in_dim(block, 0, width, axis=dim), axis, backward)
        block = jnp.concatenate([low, block, high_side], axis=dim)
    return block


def matmul(left, right):
    return jnp.dot(left, right, precision=high, preferred_element_type=jnp.float32)


def exact_matmul(left, right):
    return jnp.dot(
        left.astype(jnp.bfloat16),
        right.astype(jnp.bfloat16),
        preferred_element_type=jnp.float32,
    )


def onehot(values, count, base=0):
    return ((values - base)[..., None] == jnp.arange(count, dtype=jnp.int32)).astype(jnp.float32)


def phase_table(start, count, polar):
    order = start + jnp.arange(count, dtype=jnp.int32)
    cycle = order // (2 * polar)
    beside_all = order % (2 * polar)
    theta = math.pi * (cycle.astype(jnp.float32) + 0.5) / polar
    azimuth = math.pi * beside_all.astype(jnp.float32) / polar
    along_x = jnp.sin(theta) * jnp.cos(azimuth)
    along_y = jnp.sin(theta) * jnp.sin(azimuth)
    along_z = jnp.cos(theta)
    position = jnp.arange(64, dtype=jnp.int32)
    off_x = (position % 4).astype(jnp.float32) - 1.5
    off_y = (position // 4 % 4).astype(jnp.float32) - 1.5
    off_z = (position // 16).astype(jnp.float32) - 1.5
    angle = kappa_leaf * (
        off_x[:, None] * along_x[None, :]
        + off_y[:, None] * along_y[None, :]
        + off_z[:, None] * along_z[None, :]
    )
    return (jnp.cos(angle), jnp.sin(angle), jnp.sin(theta))


def near_field(gathered, local, kinds, near_blocks):
    count = near_blocks.shape[0]
    leaves = local.shape[0]
    width = gathered.shape[0]
    pairs = jnp.einsum(
        "ljt,ljm->tlm",
        onehot(kinds, count).astype(jnp.bfloat16),
        onehot(local, width).astype(jnp.bfloat16),
        preferred_element_type=jnp.float32,
    )
    summed = matmul(pairs.reshape(count * leaves, width), gathered.reshape(width, -1))
    summed = summed.reshape(count, leaves, 2, -1)
    block_r = near_blocks[:, 0]
    block_i = near_blocks[:, 1]

    def apply(block, rows):
        return jnp.einsum("tmn,tln->lm", block, rows, precision=high)

    real = apply(block_r, summed[:, :, 0]) - apply(block_i, summed[:, :, 1])
    imag = apply(block_r, summed[:, :, 1]) + apply(block_i, summed[:, :, 0])
    return jnp.stack([real, imag], 1)


def radiate(cur, radiation):
    real = matmul(cur[:, 0], radiation[0]) - matmul(cur[:, 1], radiation[1])
    imag = matmul(cur[:, 0], radiation[1]) + matmul(cur[:, 1], radiation[0])
    return jnp.stack([real, imag], 1)


def receive(real, imag, radiation):
    out_r = matmul(real, radiation[0].T) + matmul(imag, radiation[1].T)
    out_i = matmul(imag, radiation[0].T) - matmul(real, radiation[1].T)
    return jnp.stack([out_r, out_i], 1)


def ranks(present):
    size = present.shape[1]
    order = jnp.arange(size)
    before = (order[:, None] < order[None, :]).astype(jnp.float32)
    return exact_matmul(present, before)


def exchange_kernel(
    peers, boxes, length, index_ref, off_ref, send_ref, table_ref, out_ref, held, send_sem, recv_sem
):
    me = lax.axis_index("box")
    barrier = pltpu.get_barrier_semaphore()
    for step in range(1, peers):
        other = lax.rem(me + step, peers)
        pl.semaphore_signal(barrier, inc=1, device_id={"box": other}, device_id_type=MESH)
    pl.semaphore_wait(barrier, peers - 1)
    copies = []
    for step in range(1, peers):
        other = lax.rem(me + step, peers)
        copy = pltpu.make_async_remote_copy(
            src_ref=send_ref.at[other],
            dst_ref=held.at[me],
            send_sem=send_sem.at[step],
            recv_sem=recv_sem.at[step],
            device_id={"box": other},
            device_id_type=MESH,
        )
        copy.start()
        copies.append(copy)
    held[me] = send_ref[me]
    for copy in copies:
        copy.wait()

    def one(box, carry):
        real = jnp.zeros(out_ref.shape[2:], jnp.float32)
        imag = jnp.zeros(out_ref.shape[2:], jnp.float32)

        def entry(item, total):
            real, imag = total
            source = index_ref[box * length + item]
            off = off_ref[box * length + item]
            src_r = held[source // need, source % need, 0]
            src_i = held[source // need, source % need, 1]
            tab_r = table_ref[off, 0]
            tab_i = table_ref[off, 1]
            real = real + (tab_r * src_r - tab_i * src_i)
            imag = imag + (tab_r * src_i + tab_i * src_r)
            return real, imag

        real, imag = lax.fori_loop(0, length, entry, (real, imag), unroll=8)
        out_ref[box, 0] = real
        out_ref[box, 1] = imag
        return carry

    lax.fori_loop(0, boxes, one, 0)


def exchange(send, table, index, offsets, boxes):
    peers = send.shape[0]
    length = index.shape[0] // boxes
    tail = send.shape[2:]
    return pl.pallas_call(
        functools.partial(exchange_kernel, peers, boxes, length),
        out_shape=jax.ShapeDtypeStruct((boxes,) + tail, jnp.float32),
        in_specs=[
            pl.BlockSpec(memory_space=pltpu.SMEM),
            pl.BlockSpec(memory_space=pltpu.SMEM),
            pl.BlockSpec(memory_space=pltpu.VMEM),
            pl.BlockSpec(memory_space=pltpu.VMEM),
        ],
        out_specs=pl.BlockSpec(memory_space=pltpu.VMEM),
        scratch_shapes=[
            pltpu.VMEM(send.shape, jnp.float32),
            pltpu.SemaphoreType.DMA((peers,)),
            pltpu.SemaphoreType.DMA((peers,)),
        ],
        compiler_params=pltpu.CompilerParams(
            collective_id=0, has_side_effects=True, vmem_limit_bytes=24 * 2**20
        ),
    )(index, offsets, send, table)


def on_device(
    currents,
    near_blocks,
    block_ids,
    neighbors,
    leaf_place,
    radiation,
    interpolation,
    translation,
    list_src,
    list_offset,
):
    leaf_count = currents.shape[0]
    count_k0 = interpolation.shape[0]
    count_k1 = interpolation.shape[1]
    polar = math.isqrt(count_k1 // 2)
    scale = math.sqrt(count_k0 / count_k1)
    k1_dev = translation.shape[0]
    rows = k1_dev // 128
    nboxes = lax.axis_size("box")
    boxes = list_src.shape[0] // nboxes
    me = lax.axis_index("box")
    box_base = me * boxes
    k_base = lax.axis_index("dir") * k1_dev

    pattern = lax.all_gather(radiate(currents, radiation), "dir", axis=0, tiled=True)
    place = lax.all_gather(leaf_place, "dir", axis=0, tiled=True)
    gathered = padded(currents, ((("box", "dir"), 0),), leaf_count)
    local = neighbors - (lax.axis_index(("box", "dir")) - 1) * leaf_count
    near = near_field(gathered, local, block_ids, near_blocks)
    table = jnp.transpose(translation, (2, 1, 0)).reshape(-1, 2, rows, 128)
    part = lax.dynamic_slice_in_dim(interpolation, k_base, k1_dev, 1)
    table_c, table_s, polar_sine = phase_table(k_base, k1_dev, polar)

    named = onehot(list_src.reshape(nboxes, -1), boxes, box_base).max(1)
    slot = onehot(ranks(named).astype(jnp.int32), need) * named[:, :, None]
    slot = jnp.swapaxes(slot, 1, 2).reshape(nboxes * need, boxes)
    mine_src = lax.dynamic_slice_in_dim(list_src, box_base, boxes, 0).reshape(-1)
    mine_off = lax.dynamic_slice_in_dim(list_offset, box_base, boxes, 0).reshape(-1)
    mine_hot = onehot(mine_src, nboxes * boxes)
    wanted = mine_hot.max(0).reshape(nboxes, boxes)
    where = ranks(wanted) + need * jnp.arange(nboxes, dtype=jnp.float32)[:, None]
    mine_index = exact_matmul(mine_hot, where.reshape(-1, 1))[:, 0].astype(jnp.int32)

    parent_hot = onehot(place[:, 0], boxes, box_base)
    position_hot = onehot(place[:, 1], 64)
    cosine = matmul(position_hot, table_c)
    sine = matmul(position_hot, table_s)
    wave_r = matmul(pattern[:, 0], part)
    wave_i = matmul(pattern[:, 1], part)
    shift_r = wave_r * cosine + wave_i * sine
    shift_i = wave_i * cosine - wave_r * sine
    slot_hot = exact_matmul(slot, parent_hot.T)
    send = jnp.stack([matmul(slot_hot, shift_r), matmul(slot_hot, shift_i)], 1)
    send = send.reshape(nboxes, need, 2, rows, 128)
    fields = exchange(send, table, mine_index, mine_off, boxes)
    fields = fields.reshape(boxes, 2, k1_dev)
    field_r = matmul(parent_hot, fields[:, 0])
    field_i = matmul(parent_hot, fields[:, 1])
    weight = polar_sine * scale
    back_r = (field_r * cosine - field_i * sine) * weight
    back_i = (field_r * sine + field_i * cosine) * weight
    far = jnp.stack([matmul(back_r, part.T), matmul(back_i, part.T)], 1)
    far = lax.psum_scatter(far, "dir", scatter_dimension=0, tiled=True)
    return near + receive(far[:, 0], far[:, 1], radiation)


def solution(mesh):
    placed = (
        P(("box", "dir"), None, None),
        P(),
        P(("box", "dir"), None),
        P(("box", "dir"), None),
        P(("box", "dir"), None),
        P(),
        P(),
        P("dir", None, None),
        P(),
        P(),
    )
    return jax.shard_map(
        on_device,
        mesh=mesh,
        in_specs=placed,
        out_specs=P(("box", "dir"), None, None),
        check_vma=False,
    )
```

time: 489 us -> 167 us (0.34)
  local copies, waits for them, and re-layouts: 166 us -> 17.4 us
  other arithmetic: 89.2 us -> 1.86 us
  waiting for transfers between devices: 92.9 us -> 14.6 us
  matrix products: 115 us -> 54.6 us
  Pallas kernels: 0 us -> 42.1 us
  blocking collectives: 0 us -> 15.1 us
    gather x11 -> x0, local copies, waits for them, and re-layouts: 144 us -> none  [the longest x5 67.3 us: block(): table = jnp.take(translation, offs, axis=2)]
    dot_general x21 -> x28, matrix products: 115 us -> 54.6 us  [the longest x19 48.6 us: matmul(): jnp.dot(left, right, precision=high, preferred_element_type=jnp.float32)]
    all_gather x2 -> x0, waiting for transfers between devices: 52.3 us -> none  [the longest x1 47 us: on_device(): everything = lax.all_gather(coarse, 'box', axis=2, tiled=True)]
    select_n x20 -> x0, other arithmetic: 51.6 us -> none  [the longest x10 30.4 us: block(): table = jnp.take(translation, offs, axis=2)]
    pallas_call x0 -> x1, Pallas kernels: none -> 42.1 us  [exchange(): pl.pallas_call(functools.partial(exchange_kernel, peers, boxes, length),...]
    sub x6 -> x4, other arithmetic: 28.8 us -> 0.02 us  [the longest x1 0.01 us: phase_table(): off_y = (position // 4 % 4).astype(jnp.float32) - 1.5]
    reduce_scatter x1, waiting for transfers between devices: 36.2 us -> 14.5 us  [on_device(): far = lax.psum_scatter(far, 'dir', scatter_dimension=0, tiled=True)]
    all_gather x0 -> x2, blocking collectives: none -> 15.1 us  [the longest x1 8.46 us: on_device(): lax.all_gather(radiate(currents, radiation), 'dir', axis=0, tiled=True)]
  transfers between devices with their start and end apart: 5 -> 3, of which waited for: 5 -> 1; matrix products, arithmetic and copies ran while one was open for 4% -> 38% of each run, Pallas kernels for 0% -> 26%
where the time goes in v1:
time: 167 us; the launch traced here: 165 us
  matrix products  54.6 us (33%)
  Pallas kernels  42.1 us (25%)
  local copies, waits for them, and re-layouts  17.4 us (10%)
  blocking collectives  15.1 us (9%)
  waiting for transfers between devices  14.6 us (9%)
  between operations  13.9 us (8%)
  starting transfers between devices  5.28 us (3%)
  other arithmetic  1.86 us (1%)
    dot_general x19, matrix products, matmul(): jnp.dot(left, right, precision=high, preferred_element_type=jnp.float32)  48.6 us
    pallas_call x1, Pallas kernels, exchange(): pl.pallas_call(functools.partial(exchange_kernel, peers, boxes, length),...  42.1 us
    reduce_scatter x1, waiting for transfers between devices, on_device(): far = lax.psum_scatter(far, 'dir', scatter_dimension=0, tiled=True)  14.5 us
    all_gather x1, blocking collectives, on_device(): lax.all_gather(radiate(currents, radiation), 'dir', axis=0, tiled=True)  8.46 us
    reshape x1, local copies, waits for them, and re-layouts, on_device(): table = jnp.transpose(translation, (2, 1, 0)).reshape(-1, 2, rows, 128)  8.19 us
    all_gather x1, blocking collectives, on_device(): place = lax.all_gather(leaf_place, 'dir', axis=0, tiled=True)  6.6 us
    unnamed x31, local copies, waits for them, and re-layouts  6.5 us
  transfers between devices with their start and end apart: 3, of which 1 were waited for; matrix products, arithmetic and copies ran while one was open for 38% of the time, Pallas kernels for 26%

profile of v1, /device:TPU:27, one launch (start us, length us, event | category | flops | bytes accessed | tf_op | source)
XLA Modules:
  0.0 164.8 jit_solution(16424384844612987881)
XLA Ops:
  6.5 3.1 %collective-permute-start = (f32[128,2,128]{2,1,0:T(2,128)}, f32[128,2,128]{2,1,0:T(2,128)S(1)}, u32[]{:S(2)}, u32[]{:S(2)}) collective-permute-start(f32[128,2,128]{2,1,0:T(2,128)} %param.10), channel_id=1, source_target_pairs={{0,1},{1,2},{2,3},{3,4},{4,5},{5,6},{6,7},{7,8},{8,9},{9,10},{10,1... | collective-permute-start | bytes 393224 | tf_op jit(solution)/shard_map/ppermute | solution.py:22
  9.7 2.2 %collective-permute-start.1 = (f32[128,2,128]{2,1,0:T(2,128)}, f32[128,2,128]{2,1,0:T(2,128)S(1)}, u32[]{:S(2)}, u32[]{:S(2)}) collective-permute-start(f32[128,2,128]{2,1,0:T(2,128)} %param.10), channel_id=1, source_target_pairs={{1,0},{2,1},{3,2},{4,3},{5,4},{6,5},{7,6},{8,7},{9,8},{10,9},{11,1... | collective-permute-start | bytes 393224 | tf_op jit(solution)/shard_map/ppermute | solution.py:25
  12.0 6.6 %all_gather.6 = s32[512,2]{0,1:T(2,128)S(1)} all-gather(s32[128,2]{0,1:T(2,128)} %param.14), channel_id=1, replica_groups=mesh['box'=8,'dir'=4] {'dir'}, dimensions={0}, use_global_device_ids=true | all-gather | bytes 5120 | tf_op jit(solution)/shard_map/all_gather | solution.py:210
  18.6 4.8 %fusion.61 = f32[512,2048]{1,0:T(8,128)} fusion(f32[2048]{0:T(1024)S(1)} %fusion.129, f32[64]{0:T(128)S(1)} %get-tuple-element.11, f32[2048]{0:T(1024)S(1)} %get-tuple-element.15, f32[64]{0:T(128)S(1)} %fusion.141, f32[2048]{0:T(1024)S(1)} %get-tuple-element.16, f32[64]{0:T(128)S(1)} %get-tuple-element.12, s32[512]{0:T(512)S(1)} %bitcast.153), kind=kOutput, calls=%fused_computation.79 | convolution fusion | flops 403472384 | bytes 4221696 | tf_op jit(solution)/shard_map/dot_general | solution.py:31
  23.4 4.8 %fusion.63 = f32[512,2048]{1,0:T(8,128)} fusion(f32[2048]{0:T(1024)S(1)} %fusion.129, f32[64]{0:T(128)S(1)} %get-tuple-element.11, f32[2048]{0:T(1024)S(1)} %get-tuple-element.15, f32[64]{0:T(128)S(1)} %fusion.141, f32[2048]{0:T(1024)S(1)} %get-tuple-element.16, f32[64]{0:T(128)S(1)} %get-tuple-element.12, s32[512]{0:T(512)S(1)} %bitcast.154), kind=kOutput, calls=%fused_computation.81 | convolution fusion | flops 403472384 | bytes 4221696 | tf_op jit(solution)/shard_map/dot_general | solution.py:31
  29.1 8.5 %all_gather.7 = f32[512,2,128]{2,0,1:T(8,128)S(1)} all-gather(f32[128,2,128]{2,0,1:T(8,128)S(1)} %pad_maximum_fusion.3), channel_id=1, replica_groups=mesh['box'=8,'dir'=4] {'dir'}, dimensions={0}, use_global_device_ids=true | all-gather | bytes 655360 | tf_op jit(solution)/shard_map/all_gather | solution.py:209
  37.5 5.0 %fusion.56 = f32[512,2048]{1,0:T(8,128)} fusion(f32[128,8192]{1,0:T(8,128)} %param.16, s32[]{:T(128)S(6)} %select_n.74, f32[512,2,128]{2,0,1:T(8,128)S(1)} %all_gather.7), kind=kOutput, calls=%fused_computation.71 | convolution fusion | flops 805306368 | bytes 5505028 | tf_op jit(solution)/shard_map/dot_general | solution.py:31
  42.5 5.0 %fusion.58 = f32[512,2048]{1,0:T(8,128)} fusion(f32[128,8192]{1,0:T(8,128)} %param.16, s32[]{:T(128)S(6)} %select_n.74, f32[512,2,128]{2,0,1:T(8,128)S(1)} %all_gather.7), kind=kOutput, calls=%fused_computation.73 | convolution fusion | flops 805306368 | bytes 5505028 | tf_op jit(solution)/shard_map/dot_general | solution.py:31
  48.4 7.8 %fusion.28 = f32[8,8,16,128]{3,1,2,0:T(8,128)S(1)} fusion(f32[64,512]{1,0:T(8,128)S(1)} %fusion.111, f32[512,2048]{1,0:T(8,128)} %fusion.58, f32[512,2048]{1,0:T(8,128)} %fusion.61, f32[512,2048]{1,0:T(8,128)} %fusion.56, f32[512,2048]{1,0:T(8,128)} %fusion.63), kind=kOutput, calls=%fused_computation.33 | convolution fusion | flops 405798912 | bytes 17432576 | tf_op jit(solution)/shard_map/dot_general | solution.py:31
  56.7 1.2 copy-done.5
  57.9 1.2 copy-done.6
  59.1 2.0 %fusion.25 = f32[8,8,16,128]{3,1,2,0:T(8,128)S(1)} fusion(f32[64,512]{1,0:T(8,128)S(1)} %fusion.111, f32[512,2048]{1,0:T(8,128)S(1)} %copy-done.5, f32[512,2048]{1,0:T(8,128)S(1)} %copy-done.1, f32[512,2048]{1,0:T(8,128)S(1)} %copy-done.6, f32[512,2048]{1,0:T(8,128)S(1)} %copy-done.3), kind=kOutput, calls=%fused_computation.32 | convolution fusion | flops 405798912 | bytes 17432576 | tf_op jit(solution)/shard_map/dot_general | solution.py:31
  62.7 8.2 %reshape.155.table_ref = f32[316,2,16,128]{3,2,1,0:T(8,128)} reshape(f32[316,2,2048]{2,1,0:T(2,128)} %bitcast.143) | data formatting | bytes 10354688 | tf_op jit(solution)/shard_map/reshape | solution.py:214
  71.0 2.5 %copy-done = f32[316,2,16,128]{3,2,1,0:T(8,128)S(1)} copy-done((f32[316,2,16,128]{3,2,1,0:T(8,128)S(1)}, f32[316,2,16,128]{3,2,1,0:T(8,128)}, u32[]{:S(2)}) %copy-start) | copy-done | bytes 5177368
  73.5 42.1 %shard_map.100 = f32[32,2,16,128]{3,2,1,0:T(8,128)S(1)} custom-call(s32[1280]{0:T(1024)S(1)} %convert_element_type.128.index_ref, s32[1280]{0:T(1024)S(1)} %reshape.154.off_ref, f32[8,8,2,16,128]{4,3,2,1,0:T(8,128)S(1)} %pad_maximum_fusion.send_ref, f32[316,2,16,128]{3,2,1,0:T(8,128)S(1)} %copy-done), custom_call_target="tpu_custom_call" | custom-call | tf_op jit(solution)/shard_map/pallas_call | solution.py:163
  116.3 1.3 fusion.70
  117.7 1.3 fusion.67
  119.0 0.8 copy-done.4
  119.8 3.7 %fusion.31 = f32[512,1,128]{2,0,1:T(8,128)S(1)} fusion(f32[512,2048]{1,0:T(8,128)S(1)} %fusion.67, f32[512,2048]{1,0:T(8,128)S(1)} %copy-done.2, f32[512,2048]{1,0:T(8,128)S(1)} %fusion.70, f32[512,2048]{1,0:T(8,128)S(1)} %copy-done.4, f32[2048]{0:T(1024)S(1)} %broadcast_multiply_fusion, f32[128,8192]{1,0:T(8,128)} %param.16, s32[]{:T(128)S(6)} %select_n.74), kind=kOutput, calls=%fused_computation.34 | convolution fusion | flops 809500672 | bytes 18096132 | tf_op jit(solution)/shard_map/dot_general | solution.py:31
  123.5 3.7 %fusion.34 = f32[512,1,128]{2,0,1:T(8,128)S(1)} fusion(f32[512,2048]{1,0:T(8,128)S(1)} %fusion.67, f32[512,2048]{1,0:T(8,128)S(1)} %copy-done.4, f32[512,2048]{1,0:T(8,128)S(1)} %fusion.70, f32[512,2048]{1,0:T(8,128)S(1)} %copy-done.2, f32[2048]{0:T(1024)S(1)} %broadcast_multiply_fusion, f32[128,8192]{1,0:T(8,128)} %param.16, s32[]{:T(128)S(6)} %select_n.74), kind=kOutput, calls=%fused_computation.35 | convolution fusion | flops 809500672 | bytes 18096132 | tf_op jit(solution)/shard_map/dot_general | solution.py:31
  127.2 0.8 pad_maximum_fusion.1
  128.3 2.8 %fusion.24 = f32[16,128,384,1]{2,0,1,3:T(8,128)} fusion(s32[128,27]{1,0:T(8,128)S(1)} %copy.26, s32[128,27]{1,0:T(8,128)S(1)} %copy.27), kind=kOutput, calls=%fused_computation.26 | convolution fusion | flops 46614528 | bytes 3173376 | tf_op jit(solution)/shard_map/ljt,ljm->tlm/dot_general | solution.py:71
  131.5 4.5 %fusion.19 = f32[16,128,2,128]{3,1,2,0:T(8,128)S(1)} fusion(f32[16,128,384,1]{2,0,1,3:T(8,128)} %fusion.24, f32[384,2,128]{0,2,1:T(8,128)S(1)} %copy.39), kind=kOutput, calls=%fused_computation.21 | convolution fusion | flops 1207959552 | bytes 5636096 | tf_op jit(solution)/shard_map/dot_general | solution.py:31
  136.0 0.6 convolution_bitcast_fusion.2
  136.6 0.6 convolution_bitcast_fusion
  137.8 0.6 fusion.44
  138.4 14.5 %reduce-scatter.2.cloned.1.call-done = f32[128,2,128]{2,0,1:T(8,128)} async-done(((f32[512,2,128]{2,0,1:T(8,128)}), f32[128,2,128]{2,0,1:T(8,128)}) %reduce-scatter.2.cloned.1.call-update) | async-done | bytes 131088 | tf_op jit(solution)/shard_map/reduce_scatter | solution.py:247
  153.0 1.0 fusion.98
  154.0 1.0 fusion.96
  155.1 1.0 fusion.38
  156.1 1.0 fusion.37
  157.2 0.8 copy.35
  (72 shorter events, 6.0 us)
Async XLA Ops:
  6.5 146.4 %reduce-scatter.2.cloned.1.call-start = ((), (), s32[]{:S(2)}) async-start(), calls=%async_computation.1 | async-start | bytes 655360 | tf_op jit(solution)/shard_map/reduce_scatter | solution.py:247
  6.5 124.6 %collective-permute-start = (f32[128,2,128]{2,1,0:T(2,128)}, f32[128,2,128]{2,1,0:T(2,128)S(1)}, u32[]{:S(2)}, u32[]{:S(2)}) collective-permute-start(f32[128,2,128]{2,1,0:T(2,128)} %param.10), channel_id=1, source_target_pairs={{0,1},{1,2},{2,3},{3,4},{4,5},{5,6},{6,7},{7,8},{8,9},{9,10},{10,1... | collective-permute-start | bytes 393224 | tf_op jit(solution)/shard_map/ppermute | solution.py:22
  9.7 121.5 %collective-permute-start.1 = (f32[128,2,128]{2,1,0:T(2,128)}, f32[128,2,128]{2,1,0:T(2,128)S(1)}, u32[]{:S(2)}, u32[]{:S(2)}) collective-permute-start(f32[128,2,128]{2,1,0:T(2,128)} %param.10), channel_id=1, source_target_pairs={{1,0},{2,1},{3,2},{4,3},{5,4},{6,5},{7,6},{8,7},{9,8},{10,9},{11,1... | collective-permute-start | bytes 393224 | tf_op jit(solution)/shard_map/ppermute | solution.py:25
  18.6 9.6 %copy-start.9 = (f32[128,2,128]{2,1,0:T(2,128)S(1)}, f32[128,2,128]{2,1,0:T(2,128)}, u32[]{:S(2)}) copy-start(f32[128,2,128]{2,1,0:T(2,128)} %param.10) | copy-start | bytes 393220
  18.6 9.7 %copy-start.8 = (f32[2,128,128]{2,1,0:T(8,128)S(1)}, f32[2,128,128]{2,1,0:T(8,128)}, u32[]{:S(2)}) copy-start(f32[2,128,128]{2,1,0:T(8,128)} %param.15) | copy-start | bytes 393220
  37.5 10.0 %copy-start.10 = (s32[256,40]{0,1:T(8,128)S(1)}, s32[256,40]{0,1:T(8,128)}, u32[]{:S(2)}) copy-start(s32[256,40]{0,1:T(8,128)} %param.18) | copy-start | bytes 122884
  48.4 7.8 %copy-start.1 = (f32[512,2048]{1,0:T(8,128)S(1)}, f32[512,2048]{1,0:T(8,128)}, u32[]{:S(2)}) copy-start(f32[512,2048]{1,0:T(8,128)} %fusion.61) | copy-start | bytes 12582916
  48.4 8.3 %copy-start.3 = (f32[512,2048]{1,0:T(8,128)S(1)}, f32[512,2048]{1,0:T(8,128)}, u32[]{:S(2)}) copy-start(f32[512,2048]{1,0:T(8,128)} %fusion.63) | copy-start | bytes 12582916
  48.4 9.5 %copy-start.5 = (f32[512,2048]{1,0:T(8,128)S(1)}, f32[512,2048]{1,0:T(8,128)}, u32[]{:S(2)}) copy-start(f32[512,2048]{1,0:T(8,128)} %fusion.56) | copy-start | bytes 12582916
  48.4 10.7 %copy-start.6 = (f32[512,2048]{1,0:T(8,128)S(1)}, f32[512,2048]{1,0:T(8,128)}, u32[]{:S(2)}) copy-start(f32[512,2048]{1,0:T(8,128)} %fusion.58) | copy-start | bytes 12582916
  59.1 2.3 %copy-start.13 = (s32[256,40]{0,1:T(8,128)S(1)}, s32[256,40]{0,1:T(8,128)}, u32[]{:S(2)}) copy-start(s32[256,40]{0,1:T(8,128)} %param.19) | copy-start | bytes 122884
  71.0 2.5 %copy-start = (f32[316,2,16,128]{3,2,1,0:T(8,128)S(1)}, f32[316,2,16,128]{3,2,1,0:T(8,128)}, u32[]{:S(2)}) copy-start(f32[316,2,16,128]{3,2,1,0:T(8,128)} %reshape.155.table_ref) | copy-start | bytes 15532036
  116.3 2.6 %copy-start.2 = (f32[512,2048]{1,0:T(8,128)S(1)}, f32[512,2048]{1,0:T(8,128)}, u32[]{:S(2)}) copy-start(f32[512,2048]{1,0:T(8,128)} %fusion.61) | copy-start | bytes 12582916
  116.3 3.5 %copy-start.4 = (f32[512,2048]{1,0:T(8,128)S(1)}, f32[512,2048]{1,0:T(8,128)}, u32[]{:S(2)}) copy-start(f32[512,2048]{1,0:T(8,128)} %fusion.63) | copy-start | bytes 12582916
  123.5 4.6 %copy-start.12 = (s32[128,27]{0,1:T(8,128)S(1)}, s32[128,27]{0,1:T(8,128)}, u32[]{:S(2)}) copy-start(s32[128,27]{0,1:T(8,128)} %param.13) | copy-start | bytes 41476
  123.5 4.7 %copy-start.11 = (s32[128,27]{0,1:T(8,128)S(1)}, s32[128,27]{0,1:T(8,128)}, u32[]{:S(2)}) copy-start(s32[128,27]{0,1:T(8,128)} %param.12) | copy-start | bytes 41476
  131.1 4.9 %copy-start.7 = (f32[16,2,128,128]{3,2,1,0:T(8,128)S(1)}, f32[16,2,128,128]{3,2,1,0:T(8,128)}, u32[]{:S(2)}) copy-start(f32[16,2,128,128]{3,2,1,0:T(8,128)} %param.11) | copy-start | bytes 6291460
Sparse Core Ops, SparseCore 0:
  128.2 24.7 reduce-scatter.1

commit v2 on v1

v2 whole, which is shorter than its diff:
```python
import functools
import math

import jax
import jax.numpy as jnp
from jax import lax
from jax.experimental import pallas as pl
from jax.experimental.pallas import tpu as pltpu
from jax.sharding import PartitionSpec as P

kappa_leaf = math.pi
need = 8
MESH = pl.DeviceIdType.MESH


def exact_matmul(left, right):
    return jnp.dot(
        left.astype(jnp.bfloat16),
        right.astype(jnp.bfloat16),
        preferred_element_type=jnp.float32,
    )


def onehot(values, count, base=0):
    return ((values - base)[..., None] == jnp.arange(count, dtype=jnp.int32)).astype(jnp.float32)


def axis_factors(start, count, polar, scale):
    order = start + jnp.arange(count, dtype=jnp.int32)
    cycle = order // (2 * polar)
    beside_all = order % (2 * polar)
    theta = math.pi * (cycle.astype(jnp.float32) + 0.5) / polar
    azimuth = math.pi * beside_all.astype(jnp.float32) / polar
    along = jnp.stack(
        [jnp.sin(theta) * jnp.cos(azimuth), jnp.sin(theta) * jnp.sin(azimuth), jnp.cos(theta)]
    )
    near_angle = kappa_leaf * 0.5 * along
    far_angle = kappa_leaf * 1.5 * along
    weight = (jnp.sin(theta) * scale)[None, :]
    return jnp.concatenate(
        [jnp.cos(near_angle), jnp.sin(near_angle), jnp.cos(far_angle), jnp.sin(far_angle)]
        + [weight] * 4
    )


def near_pairs(local, kinds, count, width):
    return jnp.einsum(
        "ljt,ljm->tlm",
        onehot(kinds, count).astype(jnp.bfloat16),
        onehot(local, width).astype(jnp.bfloat16),
        preferred_element_type=jnp.float32,
    ).astype(jnp.bfloat16)


def ranks(present):
    size = present.shape[1]
    order = jnp.arange(size)
    before = (order[:, None] < order[None, :]).astype(jnp.float32)
    return exact_matmul(present, before)


nn = (((1,), (0,)), ((), ()))
nt = (((1,), (1,)), ((), ()))
tn = (((0,), (0,)), ((), ()))


def dot(left, right, dims):
    return lax.dot_general(left, right, dims, preferred_element_type=jnp.float32)


def split(value):
    top = value.astype(jnp.bfloat16)
    return top, (value - top.astype(jnp.float32)).astype(jnp.bfloat16)


def dot3(left, right, dims):
    return dot(left[0], right[0], dims) + (
        dot(left[0], right[1], dims) + dot(left[1], right[0], dims)
    )


def flag(mask):
    return mask.astype(jnp.float32).astype(jnp.bfloat16)


def fmm_kernel(
    peers,
    dirs,
    boxes,
    chunks,
    index_ref,
    off_ref,
    cur_ref,
    place_ref,
    slot_ref,
    axes_ref,
    part_ref,
    table_ref,
    pairs_ref,
    block_ref,
    rad_ref,
    out_ref,
    held_cur,
    part_h,
    part_l,
    cos_tab,
    sin_tab,
    pat_h,
    pat_l,
    cos_ref,
    sin_ref,
    acc_ref,
    near_ref,
    p_ref,
    q_ref,
    far_ref,
    far_in,
    cur_send,
    cur_recv,
    halo_send,
    halo_recv,
    box_send,
    box_recv,
    far_send,
    far_recv,
    *parts,
):
    send = parts[:chunks]
    held = parts[chunks : 2 * chunks]
    swap = parts[2 * chunks : 3 * chunks]
    me = lax.axis_index("box")
    my_dir = lax.axis_index("dir")
    leaves = cur_ref.shape[0] // 2
    width = cur_ref.shape[1]
    k1_dev = part_ref.shape[1]
    size = k1_dev // chunks
    tiles = size // 128
    rows = 2 * tiles
    slots = peers * need
    length = index_ref.shape[0] // boxes
    count = pairs_ref.shape[0]

    held_cur[1 + my_dir, 0:leaves, 0:width] = cur_ref[pl.ds(0, leaves, stride=2), :]
    held_cur[1 + my_dir, 0:leaves, width : 2 * width] = cur_ref[pl.ds(1, leaves, stride=2), :]
    held_cur[1 + my_dir, leaves : leaves + 8, :] = place_ref[...]

    up = jnp.logical_and(my_dir == dirs - 1, me < peers - 1)
    down = jnp.logical_and(my_dir == 0, me > 0)
    barrier = pltpu.get_barrier_semaphore()

    def greet(device):
        pl.semaphore_signal(barrier, inc=1, device_id=device, device_id_type=MESH)

    for step in range(1, peers):
        greet({"box": lax.rem(me + step, peers)})
    for step in range(1, dirs):
        greet({"dir": lax.rem(my_dir + step, dirs)})

    @pl.when(up)
    def _():
        greet((me + 1, 0))

    @pl.when(down)
    def _():
        greet((me - 1, dirs - 1))

    sides = up.astype(jnp.int32) + down.astype(jnp.int32)
    pl.semaphore_wait(barrier, peers + dirs - 2 + sides)

    def remote(source, target, send_sem, recv_sem, device):
        return pltpu.make_async_remote_copy(
            src_ref=source,
            dst_ref=target,
            send_sem=send_sem,
            recv_sem=recv_sem,
            device_id=device,
            device_id_type=MESH,
        )

    cur_copies = []
    for step in range(1, dirs):
        copy = remote(
            held_cur.at[1 + my_dir],
            held_cur.at[1 + my_dir],
            cur_send.at[step],
            cur_recv.at[step],
            {"dir": lax.rem(my_dir + step, dirs)},
        )
        copy.start()
        cur_copies.append(copy)

    def halo_up():
        return remote(
            held_cur.at[1 + my_dir], held_cur.at[0], halo_send.at[0], halo_recv.at[0], (me + 1, 0)
        )

    def halo_down():
        return remote(
            held_cur.at[1 + my_dir],
            held_cur.at[dirs + 1],
            halo_send.at[1],
            halo_recv.at[1],
            (me - 1, dirs - 1),
        )

    @pl.when(up)
    def _():
        halo_up().start()

    @pl.when(down)
    def _():
        halo_down().start()

    top, low = split(part_ref[...])
    part_h[...] = top
    part_l[...] = low

    def table_chunk(chunk):
        cols = pl.ds(chunk * size, size)
        position = lax.broadcasted_iota(jnp.int32, (64, size), 0)

        def factor(which, axis):
            inner = jnp.logical_or(which == 1, which == 2)
            cosine = jnp.where(inner, axes_ref[axis : axis + 1, cols], axes_ref[6 + axis : 7 + axis, cols])
            sine = jnp.where(inner, axes_ref[3 + axis : 4 + axis, cols], axes_ref[9 + axis : 10 + axis, cols])
            return cosine, jnp.where(which < 2, -sine, sine)

        x_c, x_s = factor(position % 4, 0)
        y_c, y_s = factor(position // 4 % 4, 1)
        z_c, z_s = factor(position // 16, 2)
        xy_c = x_c * y_c - x_s * y_s
        xy_s = x_c * y_s + x_s * y_c
        cos_h, cos_l = split(xy_c * z_c - xy_s * z_s)
        sin_h, sin_l = split(xy_c * z_s + xy_s * z_c)
        cos_tab[0:64, cols] = cos_h
        cos_tab[64:128, cols] = cos_l
        sin_tab[0:64, cols] = sin_h
        sin_tab[64:128, cols] = sin_l

    for chunk in range(chunks):
        table_chunk(chunk)

    rad_r = split(rad_ref[0])
    rad_i = split(rad_ref[1])
    for copy in cur_copies:
        copy.wait()

    def patterns(d, carry):
        cur_r = split(held_cur[1 + d, 0:leaves, 0:width])
        cur_i = split(held_cur[1 + d, 0:leaves, width : 2 * width])
        real = dot3(cur_r, rad_r, nn) - dot3(cur_i, rad_i, nn)
        imag = dot3(cur_r, rad_i, nn) + dot3(cur_i, rad_r, nn)
        top, low = split(real)
        pat_h[d, 0:leaves] = top
        pat_l[d, 0:leaves] = low
        top, low = split(imag)
        pat_h[d, leaves : 2 * leaves] = top
        pat_l[d, leaves : 2 * leaves] = low
        return carry

    lax.fori_loop(0, dirs, patterns, 0)

    def block(owner):
        return pl.ds(pl.multiple_of(owner * (need * rows), need * rows), need * rows)

    box_copies = []
    for chunk in range(chunks):
        cols = pl.ds(chunk * size, size)
        acc_ref[...] = jnp.zeros_like(acc_ref)

        def outgoing(d, carry):
            wave = dot3((pat_h[d], pat_l[d]), (part_h[:, cols], part_l[:, cols]), nn)
            wave_r = wave[0:leaves]
            wave_i = wave[leaves : 2 * leaves]
            parent = held_cur[1 + d, leaves : leaves + 1, 0:width]
            place = held_cur[1 + d, leaves : leaves + 1, width : 2 * width]
            order = lax.broadcasted_iota(jnp.int32, (128, leaves), 0) % 64
            hot = flag(order.astype(jnp.float32) == place)
            cosine = dot(hot, cos_tab[:, cols], tn)
            sine = dot(hot, sin_tab[:, cols], tn)
            cos_ref[d, :, cols] = cosine
            sin_ref[d, :, cols] = sine
            slot_hot = flag(slot_ref[...] == parent)
            for part, value in enumerate(
                (wave_r * cosine + wave_i * sine, wave_i * cosine - wave_r * sine)
            ):
                top, low = split(value)
                acc_ref[part] += dot(slot_hot, top, nn) + dot(slot_hot, low, nn)
            return carry

        lax.fori_loop(0, dirs, outgoing, 0)
        for tile in range(tiles):
            for part in range(2):
                send[chunk][pl.ds(2 * tile + part, slots, stride=rows), :] = acc_ref[
                    part, :, tile * 128 : (tile + 1) * 128
                ]
        copies = []
        for step in range(1, peers):
            other = lax.rem(me + step, peers)
            copy = remote(
                send[chunk].at[block(other)],
                held[chunk].at[block(me)],
                box_send.at[chunk, step],
                box_recv.at[chunk, step],
                {"box": other},
            )
            copy.start()
            copies.append(copy)
        box_copies.append(copies)
        held[chunk][block(me), :] = send[chunk][block(me), :]

    @pl.when(up)
    def _():
        halo_up().wait_send()

    @pl.when(down)
    def _():
        halo_down().wait_send()

    @pl.when(down)
    def _():
        halo_up().wait_recv()

    @pl.when(up)
    def _():
        halo_down().wait_recv()

    @pl.when(me == 0)
    def _():
        held_cur[0] = jnp.zeros(held_cur.shape[1:], jnp.float32)

    @pl.when(me == peers - 1)
    def _():
        held_cur[dirs + 1] = jnp.zeros(held_cur.shape[1:], jnp.float32)

    around = jnp.concatenate([held_cur[my_dir + side, 0:leaves, :] for side in range(3)], axis=0)
    around_h, around_l = split(around)
    near_ref[...] = jnp.zeros_like(near_ref)

    def near(t, carry):
        summed = dot(pairs_ref[t], around_h, nn) + dot(pairs_ref[t], around_l, nn)
        stacked = split(jnp.concatenate([summed[:, 0:width], summed[:, width : 2 * width]], axis=0))
        by_r = dot3(stacked, split(block_ref[t, 0]), nt)
        by_i = dot3(stacked, split(block_ref[t, 1]), nt)
        near_ref[0] += by_r[0:leaves] - by_i[leaves : 2 * leaves]
        near_ref[1] += by_r[leaves : 2 * leaves] + by_i[0:leaves]
        return carry

    lax.fori_loop(0, count, near, 0)
    far_ref[...] = jnp.zeros_like(far_ref)

    for chunk in range(chunks):
        cols = pl.ds(chunk * size, size)
        for copy in box_copies[chunk]:
            copy.wait()
        got = held[chunk]
        other = swap[chunk]

        def turn(slot, carry):
            where = pl.ds(pl.multiple_of(slot * rows, rows), rows)
            value = got[where, :]
            odd = lax.broadcasted_iota(jnp.int32, value.shape, 0) % 2
            other[slot, 0] = value
            other[slot, 1] = jnp.where(
                odd == 0, pltpu.roll(value, rows - 1, 0), pltpu.roll(value, 1, 0)
            )
            return carry

        lax.fori_loop(0, slots, turn, 0, unroll=4)

        def translate(box, carry):
            def entry(item, total):
                along, across = total
                source = index_ref[box * length + item]
                table = table_ref[off_ref[box * length + item], chunk]
                return along + table * other[source, 0], across + table * other[source, 1]

            zero = jnp.zeros((rows, 128), jnp.float32)
            along, across = lax.fori_loop(0, length, entry, (zero, zero), unroll=8)
            where = pl.ds(pl.multiple_of(box * rows, rows), rows)
            p_ref[where, :] = along
            q_ref[where, :] = across
            return carry

        lax.fori_loop(0, boxes, translate, 0)

        def pick(ref, row):
            return ref[pl.ds(row, boxes, stride=rows), :]

        field_r = jnp.concatenate(
            [pick(p_ref, 2 * tile) - pick(p_ref, 2 * tile + 1) for tile in range(tiles)], axis=1
        )
        field_i = jnp.concatenate(
            [pick(q_ref, 2 * tile) + pick(q_ref, 2 * tile + 1) for tile in range(tiles)], axis=1
        )
        field_r = jnp.concatenate(split(field_r), axis=0)
        field_i = jnp.concatenate(split(field_i), axis=0)

        def incoming(d, carry):
            parent = held_cur[1 + d, leaves : leaves + 1, 0:width]
            order = lax.broadcasted_iota(jnp.int32, (2 * boxes, leaves), 0) % boxes + me * boxes
            hot = flag(order.astype(jnp.float32) == parent)
            real = dot(hot, field_r, tn)
            imag = dot(hot, field_i, tn)
            cosine = cos_ref[d, :, cols]
            sine = sin_ref[d, :, cols]
            weight = axes_ref[12:13, cols]
            back = (part_h[:, cols], part_l[:, cols])
            far_ref[d, 0:leaves] += dot3(split((real * cosine - imag * sine) * weight), back, nt)
            far_ref[d, leaves : 2 * leaves] += dot3(
                split((real * sine + imag * cosine) * weight), back, nt
            )
            return carry

        lax.fori_loop(0, dirs, incoming, 0)

    copies = []
    for step in range(1, dirs):
        other_dir = lax.rem(my_dir + step, dirs)
        copy = remote(
            far_ref.at[other_dir],
            far_in.at[step],
            far_send.at[step],
            far_recv.at[step],
            {"dir": other_dir},
        )
        copy.start()
        copies.append(copy)
    far = far_ref[my_dir]
    for step, copy in enumerate(copies):
        copy.wait()
        far = far + far_in[step + 1]
    far = split(far)
    by_r = dot3(far, rad_r, nt)
    by_i = dot3(far, rad_i, nt)
    out_ref[pl.ds(0, leaves, stride=2), :] = near_ref[0] + by_r[0:leaves] + by_i[leaves : 2 * leaves]
    out_ref[pl.ds(1, leaves, stride=2), :] = near_ref[1] + by_r[leaves : 2 * leaves] - by_i[0:leaves]


def fmm(peers, dirs, boxes, index, offsets, *arrays):
    cur, place, slots, axes, part, table, pairs, blocks, radiation = arrays
    k0, k1_dev = part.shape
    chunks = max(1, k1_dev // 1024)
    size = k1_dev // chunks
    rows = 2 * size // 128
    leaves = cur.shape[0] // 2
    exchanged = pltpu.VMEM((peers * need * rows, 128), jnp.float32)
    dma = pltpu.SemaphoreType.DMA
    vmem = pl.BlockSpec(memory_space=pltpu.VMEM)
    smem = pl.BlockSpec(memory_space=pltpu.SMEM)
    f32 = jnp.float32
    bf16 = jnp.bfloat16
    return pl.pallas_call(
        functools.partial(fmm_kernel, peers, dirs, boxes, chunks),
        out_shape=jax.ShapeDtypeStruct(cur.shape, f32),
        in_specs=[smem, smem] + [vmem] * len(arrays),
        out_specs=vmem,
        scratch_shapes=[
            pltpu.VMEM((dirs + 2, leaves + 8, 2 * cur.shape[1]), f32),
            pltpu.VMEM((k0, k1_dev), bf16),
            pltpu.VMEM((k0, k1_dev), bf16),
            pltpu.VMEM((128, k1_dev), bf16),
            pltpu.VMEM((128, k1_dev), bf16),
            pltpu.VMEM((dirs, 2 * leaves, k0), bf16),
            pltpu.VMEM((dirs, 2 * leaves, k0), bf16),
            pltpu.VMEM((dirs, leaves, k1_dev), f32),
            pltpu.VMEM((dirs, leaves, k1_dev), f32),
            pltpu.VMEM((2, peers * need, size), f32),
            pltpu.VMEM((2, leaves, cur.shape[1]), f32),
            pltpu.VMEM((boxes * rows, 128), f32),
            pltpu.VMEM((boxes * rows, 128), f32),
            pltpu.VMEM((dirs, 2 * leaves, k0), f32),
            pltpu.VMEM((dirs, 2 * leaves, k0), f32),
            dma((dirs,)),
            dma((dirs,)),
            dma((2,)),
            dma((2,)),
            dma((chunks, peers)),
            dma((chunks, peers)),
            dma((dirs,)),
            dma((dirs,)),
        ]
        + [exchanged] * (2 * chunks)
        + [pltpu.VMEM((peers * need, 2, rows, 128), f32)] * chunks,
        compiler_params=pltpu.CompilerParams(
            collective_id=0, has_side_effects=True, vmem_limit_bytes=50 * 2**20
        ),
    )(index, offsets, *arrays)


def on_device(
    currents,
    near_blocks,
    block_ids,
    neighbors,
    leaf_place,
    radiation,
    interpolation,
    translation,
    list_src,
    list_offset,
):
    leaf_count = currents.shape[0]
    count_k0 = interpolation.shape[0]
    count_k1 = interpolation.shape[1]
    polar = math.isqrt(count_k1 // 2)
    scale = math.sqrt(count_k0 / count_k1)
    k1_dev = translation.shape[0]
    rows = k1_dev // 128
    nboxes = lax.axis_size("box")
    boxes = list_src.shape[0] // nboxes
    me = lax.axis_index("box")
    box_base = me * boxes
    k_base = lax.axis_index("dir") * k1_dev

    local = neighbors - (lax.axis_index(("box", "dir")) - 1) * leaf_count
    pairs = near_pairs(local, block_ids, near_blocks.shape[0], 3 * leaf_count)
    table = jnp.transpose(translation, (2, 1, 0)).reshape(-1, 2, rows, 128)
    chunks = max(1, k1_dev // 1024)
    table = jnp.swapaxes(table, 1, 2).reshape(-1, chunks, 2 * rows // chunks, 128)
    part = lax.dynamic_slice_in_dim(interpolation, k_base, k1_dev, 1)
    axes = axis_factors(k_base, k1_dev, polar, scale)
    place = jnp.broadcast_to(leaf_place.T.astype(jnp.float32).reshape(1, -1), (8, 2 * leaf_count))

    named = onehot(list_src.reshape(nboxes, -1), boxes, box_base).max(1)
    slot = onehot(ranks(named).astype(jnp.int32), need) * named[:, :, None]
    slot = jnp.swapaxes(slot, 1, 2).reshape(nboxes * need, boxes)
    mine_src = lax.dynamic_slice_in_dim(list_src, box_base, boxes, 0).reshape(-1)
    mine_off = lax.dynamic_slice_in_dim(list_offset, box_base, boxes, 0).reshape(-1)
    mine_hot = onehot(mine_src, nboxes * boxes)
    wanted = mine_hot.max(0).reshape(nboxes, boxes)
    where = ranks(wanted) + need * jnp.arange(nboxes, dtype=jnp.float32)[:, None]
    mine_index = exact_matmul(mine_hot, where.reshape(-1, 1))[:, 0].astype(jnp.int32)

    named_box = exact_matmul(slot, jnp.arange(boxes, dtype=jnp.float32)[:, None]) + (
        box_base.astype(jnp.float32)
    )
    slots = jnp.broadcast_to(named_box, (nboxes * need, leaf_count))
    out = fmm(
        nboxes,
        lax.axis_size("dir"),
        boxes,
        mine_index,
        mine_off,
        currents.reshape(2 * leaf_count, -1),
        place,
        slots,
        axes,
        part,
        table,
        pairs,
        near_blocks,
        radiation,
    )
    return out.reshape(currents.shape)


def solution(mesh):
    placed = (
        P(("box", "dir"), None, None),
        P(),
        P(("box", "dir"), None),
        P(("box", "dir"), None),
        P(("box", "dir"), None),
        P(),
        P(),
        P("dir", None, None),
        P(),
        P(),
    )
    return jax.shard_map(
        on_device,
        mesh=mesh,
        in_specs=placed,
        out_specs=P(("box", "dir"), None, None),
        check_vma=False,
    )
```

time: 167 us -> 74.2 us (0.44); the launches traced: 165 us -> 73.9 us
  matrix products: 54.6 us -> 2.03 us
  Pallas kernels: 42.1 us -> 64.1 us
  blocking collectives: 15.1 us -> 0 us
  waiting for transfers between devices: 14.6 us -> 0 us
  between operations: 13.9 us -> 0.15 us
  local copies, waits for them, and re-layouts: 17.4 us -> 5.04 us
  starting transfers between devices: 5.28 us -> 0 us
    dot_general x24 -> x1, matrix products: 53.8 us -> 1.26 us  [near_pairs(): jnp.einsum('ljt,ljm->tlm', onehot(kinds, count).astype(jnp.bfloat16), one...]
    pallas_call x1, Pallas kernels: 42.1 us -> 64.1 us  [fmm(): pl.pallas_call(functools.partial(fmm_kernel, peers, dirs, boxes, chunks),...]
    all_gather x2 -> x0, blocking collectives: 15.1 us -> none  [the longest x1 8.46 us: on_device(): lax.all_gather(radiate(currents, radiation), 'dir', axis=0, tiled=True)]
    reduce_scatter x1 -> x0, waiting for transfers between devices: 14.5 us -> none  [on_device(): far = lax.psum_scatter(far, 'dir', scatter_dimension=0, tiled=True)]
    reshape x3 -> x0, local copies, waits for them, and re-layouts: 8.64 us -> none  [the longest x1 8.19 us: on_device(): table = jnp.transpose(translation, (2, 1, 0)).reshape(-1, 2, rows, 128)]
    ppermute x2 -> x0, starting transfers between devices: 5.27 us -> none  [the longest x1 3.11 us: padded(): lax.ppermute(lax.slice_in_dim(block, block.shape[dim] - width, None, axis...]
    unnamed x31 -> x12, local copies, waits for them, and re-layouts: 6.5 us -> 1.35 us
  transfers between devices with their start and end apart: 3 -> 0, of which waited for: 1 -> 0; matrix products, arithmetic and copies ran while one was open for 38% -> 0% of each run, Pallas kernels for 26% -> 0%
where the time goes in v2:
time: 74.2 us; the launch traced here: 73.9 us
  Pallas kernels  64.1 us (86%)
  local copies, waits for them, and re-layouts  5.04 us (7%)
  other arithmetic  2.61 us (4%)
  matrix products  2.03 us (3%)
    pallas_call x1, Pallas kernels, fmm(): pl.pallas_call(functools.partial(fmm_kernel, peers, dirs, boxes, chunks),...  64.1 us

profile of v2, /device:TPU:27, one launch (start us, length us, event | category | flops | bytes accessed | tf_op | source)
XLA Modules:
  0.0 73.9 jit_solution(17742410886643255580)
XLA Ops:
  0.0 0.5 sine_multiply_fusion
  0.5 0.3 broadcast_multiply_fusion
  0.8 0.5 multiply_sine_fusion
  1.3 0.3 concatenate.3.axes_ref
  1.6 0.8 %constant_dynamic-slice_fusion.1 = (s32[32,40]{0,1:T(8,128)S(1)}, s32[32,40]{0,1:T(8,128)S(1)}) fusion(s32[256,40]{0,1:T(8,128)} %param.19, s32[]{:T(128)S(6)} %select_n.49, s32[256,40]{0,1:T(8,128)} %param.18), kind=kLoop, calls=%fused_computation.53 | loop fusion | bytes 20484 | tf_op jit(solution)/shard_map/dynamic_slice | solution.py:529
  2.4 0.1 copy.22
  2.5 0.1 eq.78
  2.6 0.3 convert_reduce_fusion
  2.8 0.1 convert_element_type.144
  2.9 0.1 fusion.3
  3.0 0.1 reshape.218
  3.1 0.4 convolution_reduce_fusion
  3.6 0.8 %broadcast_subtract_fusion = s32[256,40]{0,1:T(8,128)S(1)} fusion(s32[256,40]{0,1:T(8,128)} %param.18, s32[]{:T(128)S(6)} %mul.75), kind=kLoop, calls=%fused_computation.30 | loop fusion | flops 10240 | bytes 81924 | tf_op jit(solution)/shard_map/sub | solution.py:25
  4.4 0.1 copy.24
  4.4 0.1 sub.30
  4.6 0.2 convert_reduce_fusion.1
  4.8 0.1 convolution_convert_fusion
  4.9 0.1 fusion.4
  5.1 0.1 broadcast_in_dim.8.slot_ref
  5.1 0.1 copy.23
  5.2 0.1 reshape.213.off_ref
  5.3 1.3 %constant_dynamic-slice_fusion.part_ref = f32[128,2048]{1,0:T(8,128)S(1)} fusion(f32[128,8192]{1,0:T(8,128)} %param.16, s32[]{:T(128)S(6)} %select_n.52), kind=kLoop, calls=%fused_computation.52 | loop fusion | bytes 2097156 | tf_op jit(solution)/shard_map/dynamic_slice | solution.py:521
  6.7 0.1 copy.26
  6.8 0.1 copy.27
  6.9 1.3 %fusion = bf16[128,384,16]{1,2,0:T(8,128)(2,1)S(1)} fusion(s32[128,27]{1,0:T(8,128)S(1)} %copy.26, s32[128,27]{1,0:T(8,128)S(1)} %copy.27), kind=kOutput, calls=%fused_computation.2 | convolution fusion | flops 46614528 | bytes 1600512 | tf_op jit(solution)/shard_map/ljt,ljm->tlm/dot_general | solution.py:47
  8.2 0.0 copy-start.4
  8.2 0.4 copy.32
  8.6 0.3 copy-done.4
  8.9 0.2 copy-done
  9.1 0.1 copy-done.1
  9.2 64.1 %shard_map.100 = f32[256,128]{1,0:T(8,128)S(1)} custom-call(s32[1280]{0:T(1024)S(1)} %convert_element_type.149.index_ref, s32[1280]{0:T(1024)S(1)} %reshape.213.off_ref, f32[256,128]{1,0:T(8,128)S(1)} %bitcast.29, f32[8,256]{1,0:T(8,128)S(1)} %broadcast_in_dim.7.place_ref, f32[64,128]{1,0:T(8,128)S(1)} %broadcast_in_dim.8.slot_ref, ...), custom_call_target="tpu_custom_call" | custom-call | tf_op jit(solution)/shard_map/pallas_call | solution.py:453
  73.3 0.7 copy.34
  (11 shorter events, 0.0 us)
Async XLA Ops:
  3.1 3.6 %copy-start.3 = (s32[128,27]{0,1:T(8,128)S(1)}, s32[128,27]{0,1:T(8,128)}, u32[]{:S(2)}) copy-start(s32[128,27]{0,1:T(8,128)} %param.13) | copy-start | bytes 41476
  3.1 3.7 %copy-start.2 = (s32[128,27]{0,1:T(8,128)S(1)}, s32[128,27]{0,1:T(8,128)}, u32[]{:S(2)}) copy-start(s32[128,27]{0,1:T(8,128)} %param.12) | copy-start | bytes 41476
  8.2 0.7 copy-start.4
  8.2 0.9 %copy-start = (f32[128,2,128]{2,1,0:T(2,128)S(1)}, f32[128,2,128]{2,1,0:T(2,128)}, u32[]{:S(2)}) copy-start(f32[128,2,128]{2,1,0:T(2,128)} %param.10) | copy-start | bytes 393220
  8.2 1.0 %copy-start.1 = (f32[2,128,128]{2,1,0:T(8,128)S(1)}, f32[2,128,128]{2,1,0:T(8,128)}, u32[]{:S(2)}) copy-start(f32[2,128,128]{2,1,0:T(8,128)} %rad_ref.1) | copy-start | bytes 393220

commit v3 on v2

--- a/solution.py
+++ b/solution.py
@@ -94,12 +94,16 @@
     place_ref,
     slot_ref,
     axes_ref,
+    part_hbm,
+    table_hbm,
+    pairs_ref,
+    block_hbm,
+    rad_ref,
+    out_ref,
     part_ref,
     table_ref,
-    pairs_ref,
     block_ref,
-    rad_ref,
-    out_ref,
+    load_sem,
     held_cur,
     part_h,
     part_l,
@@ -140,6 +144,13 @@
     length = index_ref.shape[0] // boxes
     count = pairs_ref.shape[0]
 
+    part_cols = pl.ds(pl.multiple_of(my_dir * k1_dev, k1_dev), k1_dev)
+    load_part = pltpu.make_async_copy(part_hbm.at[:, part_cols], part_ref, load_sem.at[0])
+    load_block = pltpu.make_async_copy(block_hbm, block_ref, load_sem.at[1])
+    load_table = pltpu.make_async_copy(table_hbm, table_ref, load_sem.at[2])
+    load_part.start()
+    load_block.start()
+    load_table.start()
     held_cur[1 + my_dir, 0:leaves, 0:width] = cur_ref[pl.ds(0, leaves, stride=2), :]
     held_cur[1 + my_dir, 0:leaves, width : 2 * width] = cur_ref[pl.ds(1, leaves, stride=2), :]
     held_cur[1 + my_dir, leaves : leaves + 8, :] = place_ref[...]
@@ -211,6 +222,7 @@
     def _():
         halo_down().start()
 
+    load_part.wait()
     top, low = split(part_ref[...])
     part_h[...] = top
     part_l[...] = low
@@ -242,10 +254,9 @@
 
     rad_r = split(rad_ref[0])
     rad_i = split(rad_ref[1])
-    for copy in cur_copies:
-        copy.wait()
-
-    def patterns(d, carry):
+    acc_ref[...] = jnp.zeros_like(acc_ref)
+
+    def patterns(d):
         cur_r = split(held_cur[1 + d, 0:leaves, 0:width])
         cur_i = split(held_cur[1 + d, 0:leaves, width : 2 * width])
         real = dot3(cur_r, rad_r, nn) - dot3(cur_i, rad_i, nn)
@@ -256,43 +267,51 @@
         top, low = split(imag)
         pat_h[d, leaves : 2 * leaves] = top
         pat_l[d, leaves : 2 * leaves] = low
-        return carry
-
-    lax.fori_loop(0, dirs, patterns, 0)
 
     def block(owner):
         return pl.ds(pl.multiple_of(owner * (need * rows), need * rows), need * rows)
 
+    def outgoing(d, chunk):
+        cols = pl.ds(chunk * size, size)
+        wave = dot3((pat_h[d], pat_l[d]), (part_h[:, cols], part_l[:, cols]), nn)
+        wave_r = wave[0:leaves]
+        wave_i = wave[leaves : 2 * leaves]
+        parent = held_cur[1 + d, leaves : leaves + 1, 0:width]
+        place = held_cur[1 + d, leaves : leaves + 1, width : 2 * width]
+        order = lax.broadcasted_iota(jnp.int32, (128, leaves), 0) % 64
+        hot = flag(order.astype(jnp.float32) == place)
+        cosine = dot(hot, cos_tab[:, cols], tn)
+        sine = dot(hot, sin_tab[:, cols], tn)
+        cos_ref[d, :, cols] = cosine
+        sin_ref[d, :, cols] = sine
+        slot_hot = flag(slot_ref[...] == parent)
+        for part, value in enumerate(
+            (wave_r * cosine + wave_i * sine, wave_i * cosine - wave_r * sine)
+        ):
+            top, low = split(value)
+            acc_ref[chunk, part] += dot(slot_hot, top, nn) + dot(slot_hot, low, nn)
+
+    patterns(my_dir)
+    for chunk in range(chunks):
+        outgoing(my_dir, chunk)
+    for copy in cur_copies:
+        copy.wait()
+
     box_copies = []
     for chunk in range(chunks):
-        cols = pl.ds(chunk * size, size)
-        acc_ref[...] = jnp.zeros_like(acc_ref)
-
-        def outgoing(d, carry):
-            wave = dot3((pat_h[d], pat_l[d]), (part_h[:, cols], part_l[:, cols]), nn)
-            wave_r = wave[0:leaves]
-            wave_i = wave[leaves : 2 * leaves]
-            parent = held_cur[1 + d, leaves : leaves + 1, 0:width]
-            place = held_cur[1 + d, leaves : leaves + 1, width : 2 * width]
-            order = lax.broadcasted_iota(jnp.int32, (128, leaves), 0) % 64
-            hot = flag(order.astype(jnp.float32) == place)
-            cosine = dot(hot, cos_tab[:, cols], tn)
-            sine = dot(hot, sin_tab[:, cols], tn)
-            cos_ref[d, :, cols] = cosine
-            sin_ref[d, :, cols] = sine
-            slot_hot = flag(slot_ref[...] == parent)
-            for part, value in enumerate(
-                (wave_r * cosine + wave_i * sine, wave_i * cosine - wave_r * sine)
-            ):
-                top, low = split(value)
-                acc_ref[part] += dot(slot_hot, top, nn) + dot(slot_hot, low, nn)
+
+        def others(step, carry):
+            d = lax.rem(my_dir + step, dirs)
+            if chunk == 0:
+                patterns(d)
+            outgoing(d, chunk)
             return carry
 
-        lax.fori_loop(0, dirs, outgoing, 0)
+        lax.fori_loop(1, dirs, others, 0)
         for tile in range(tiles):
             for part in range(2):
                 send[chunk][pl.ds(2 * tile + part, slots, stride=rows), :] = acc_ref[
-                    part, :, tile * 128 : (tile + 1) * 128
+                    chunk, part, :, tile * 128 : (tile + 1) * 128
                 ]
         copies = []
         for step in range(1, peers):
@@ -346,7 +365,9 @@
         near_ref[1] += by_r[leaves : 2 * leaves] + by_i[0:leaves]
         return carry
 
-    lax.fori_loop(0, count, near, 0)
+    load_block.wait()
+    lax.fori_loop(0, count // 2, near, 0)
+    load_table.wait()
     far_ref[...] = jnp.zeros_like(far_ref)
 
     for chunk in range(chunks):
@@ -396,7 +417,7 @@
         field_r = jnp.concatenate(split(field_r), axis=0)
         field_i = jnp.concatenate(split(field_i), axis=0)
 
-        def incoming(d, carry):
+        def incoming(d):
             parent = held_cur[1 + d, leaves : leaves + 1, 0:width]
             order = lax.broadcasted_iota(jnp.int32, (2 * boxes, leaves), 0) % boxes + me * boxes
             hot = flag(order.astype(jnp.float32) == parent)
@@ -410,13 +431,18 @@
             far_ref[d, leaves : 2 * leaves] += dot3(
                 split((real * sine + imag * cosine) * weight), back, nt
             )
+
+        def all_incoming(d, carry):
+            incoming(d)
             return carry
 
-        lax.fori_loop(0, dirs, incoming, 0)
+        if chunk < chunks - 1:
+            lax.fori_loop(0, dirs, all_incoming, 0)
 
     copies = []
     for step in range(1, dirs):
         other_dir = lax.rem(my_dir + step, dirs)
+        incoming(other_dir)
         copy = remote(
             far_ref.at[other_dir],
             far_in.at[step],
@@ -426,6 +452,8 @@
         )
         copy.start()
         copies.append(copy)
+    incoming(my_dir)
+    lax.fori_loop(count // 2, count, near, 0)
     far = far_ref[my_dir]
     for step, copy in enumerate(copies):
         copy.wait()
@@ -439,7 +467,8 @@
 
 def fmm(peers, dirs, boxes, index, offsets, *arrays):
     cur, place, slots, axes, part, table, pairs, blocks, radiation = arrays
-    k0, k1_dev = part.shape
+    k0 = part.shape[0]
+    k1_dev = part.shape[1] // dirs
     chunks = max(1, k1_dev // 1024)
     size = k1_dev // chunks
     rows = 2 * size // 128
@@ -448,14 +477,19 @@
     dma = pltpu.SemaphoreType.DMA
     vmem = pl.BlockSpec(memory_space=pltpu.VMEM)
     smem = pl.BlockSpec(memory_space=pltpu.SMEM)
+    hbm = pl.BlockSpec(memory_space=pl.ANY)
     f32 = jnp.float32
     bf16 = jnp.bfloat16
     return pl.pallas_call(
         functools.partial(fmm_kernel, peers, dirs, boxes, chunks),
         out_shape=jax.ShapeDtypeStruct(cur.shape, f32),
-        in_specs=[smem, smem] + [vmem] * len(arrays),
+        in_specs=[smem, smem] + [vmem] * 4 + [hbm, hbm, vmem, hbm, vmem],
         out_specs=vmem,
         scratch_shapes=[
+            pltpu.VMEM((k0, k1_dev), f32),
+            pltpu.VMEM(table.shape, f32),
+            pltpu.VMEM(blocks.shape, f32),
+            dma((3,)),
             pltpu.VMEM((dirs + 2, leaves + 8, 2 * cur.shape[1]), f32),
             pltpu.VMEM((k0, k1_dev), bf16),
             pltpu.VMEM((k0, k1_dev), bf16),
@@ -465,7 +499,7 @@
             pltpu.VMEM((dirs, 2 * leaves, k0), bf16),
             pltpu.VMEM((dirs, leaves, k1_dev), f32),
             pltpu.VMEM((dirs, leaves, k1_dev), f32),
-            pltpu.VMEM((2, peers * need, size), f32),
+            pltpu.VMEM((chunks, 2, peers * need, size), f32),
             pltpu.VMEM((2, leaves, cur.shape[1]), f32),
             pltpu.VMEM((boxes * rows, 128), f32),
             pltpu.VMEM((boxes * rows, 128), f32),
@@ -518,7 +552,6 @@
     table = jnp.transpose(translation, (2, 1, 0)).reshape(-1, 2, rows, 128)
     chunks = max(1, k1_dev // 1024)
     table = jnp.swapaxes(table, 1, 2).reshape(-1, chunks, 2 * rows // chunks, 128)
-    part = lax.dynamic_slice_in_dim(interpolation, k_base, k1_dev, 1)
     axes = axis_factors(k_base, k1_dev, polar, scale)
     place = jnp.broadcast_to(leaf_place.T.astype(jnp.float32).reshape(1, -1), (8, 2 * leaf_count))
 
@@ -546,7 +579,7 @@
         place,
         slots,
         axes,
-        part,
+        interpolation,
         table,
         pairs,
         near_blocks,

time: 74.2 us -> 66.6 us (0.90)
  Pallas kernels: 64.1 us -> 57.5 us
  local copies, waits for them, and re-layouts: 5.04 us -> 3.71 us
    pallas_call x1, Pallas kernels: 64.1 us -> 57.5 us  [fmm(): pl.pallas_call(functools.partial(fmm_kernel, peers, dirs, boxes, chunks),...]
    dynamic_slice x1 -> x0, local copies, waits for them, and re-layouts: 1.32 us -> none  [on_device(): part = lax.dynamic_slice_in_dim(interpolation, k_base, k1_dev, 1)]
where the time goes in v3:
time: 66.6 us; the launch traced here: 66 us
  Pallas kernels  57.5 us (86%)
  local copies, waits for them, and re-layouts  3.71 us (6%)
  other arithmetic  2.61 us (4%)
  matrix products  2.03 us (3%)
    pallas_call x1, Pallas kernels, fmm(): pl.pallas_call(functools.partial(fmm_kernel, peers, dirs, boxes, chunks),...  57.5 us
    unnamed x12, local copies, waits for them, and re-layouts  1.35 us

profile of v3, /device:TPU:27, one launch (start us, length us, event | category | flops | bytes accessed | tf_op | source)
XLA Modules:
  0.0 66.0 jit_solution(65960009083985287)
XLA Ops:
  0.0 0.5 sine_multiply_fusion
  0.5 0.3 broadcast_multiply_fusion
  0.8 0.5 multiply_sine_fusion
  1.3 0.3 concatenate.3.axes_ref
  1.6 0.8 %constant_dynamic-slice_fusion = (s32[32,40]{0,1:T(8,128)S(1)}, s32[32,40]{0,1:T(8,128)S(1)}) fusion(s32[256,40]{0,1:T(8,128)} %param.19, s32[]{:T(128)S(6)} %select_n.46, s32[256,40]{0,1:T(8,128)} %param.18), kind=kLoop, calls=%fused_computation.55 | loop fusion | bytes 20484 | tf_op jit(solution)/shard_map/dynamic_slice | solution.py:562
  2.4 0.1 copy.22
  2.5 0.1 eq.78
  2.6 0.3 convert_reduce_fusion
  2.8 0.1 convert_element_type.144
  2.9 0.1 fusion.3
  3.0 0.1 reshape.218
  3.1 0.4 convolution_reduce_fusion
  3.6 0.8 %broadcast_subtract_fusion = s32[256,40]{0,1:T(8,128)S(1)} fusion(s32[256,40]{0,1:T(8,128)} %param.18, s32[]{:T(128)S(6)} %mul.75), kind=kLoop, calls=%fused_computation.30 | loop fusion | flops 10240 | bytes 81924 | tf_op jit(solution)/shard_map/sub | solution.py:25
  4.4 0.1 copy.24
  4.5 0.1 sub.30
  4.6 0.2 convert_reduce_fusion.1
  4.8 0.1 convolution_convert_fusion
  4.9 0.1 fusion.4
  5.1 0.1 broadcast_in_dim.8.slot_ref
  5.1 0.1 copy.23
  5.2 0.1 reshape.213.off_ref
  5.4 0.1 copy.26
  5.5 0.1 copy.27
  5.6 1.3 %fusion = bf16[128,384,16]{1,2,0:T(8,128)(2,1)S(1)} fusion(s32[128,27]{1,0:T(8,128)S(1)} %copy.26, s32[128,27]{1,0:T(8,128)S(1)} %copy.27), kind=kOutput, calls=%fused_computation.2 | convolution fusion | flops 46614528 | bytes 1600512 | tf_op jit(solution)/shard_map/ljt,ljm->tlm/dot_general | solution.py:47
  6.8 0.0 copy-start.4
  6.9 0.0 copy-start.1
  6.9 0.4 copy.32
  7.3 0.3 copy-done.4
  7.5 0.2 copy-done
  7.8 0.1 copy-done.1
  7.8 57.5 %shard_map.100 = f32[256,128]{1,0:T(8,128)S(1)} custom-call(s32[1280]{0:T(1024)S(1)} %convert_element_type.149.index_ref, s32[1280]{0:T(1024)S(1)} %reshape.213.off_ref, f32[256,128]{1,0:T(8,128)S(1)} %bitcast.29, f32[8,256]{1,0:T(8,128)S(1)} %broadcast_in_dim.7.place_ref, f32[64,128]{1,0:T(8,128)S(1)} %broadcast_in_dim.8.slot_ref, ...), custom_call_target="tpu_custom_call" | custom-call | tf_op jit(solution)/shard_map/pallas_call | solution.py:483
  65.3 0.7 copy.34
  (10 shorter events, 0.0 us)
Async XLA Ops:
  0.0 5.3 %copy-start.3 = (s32[128,27]{0,1:T(8,128)S(1)}, s32[128,27]{0,1:T(8,128)}, u32[]{:S(2)}) copy-start(s32[128,27]{0,1:T(8,128)} %param.13) | copy-start | bytes 41476
  0.0 5.5 %copy-start.2 = (s32[128,27]{0,1:T(8,128)S(1)}, s32[128,27]{0,1:T(8,128)}, u32[]{:S(2)}) copy-start(s32[128,27]{0,1:T(8,128)} %param.12) | copy-start | bytes 41476
  6.8 0.7 %copy-start.4 = (s32[128,2]{0,1:T(2,128)S(1)}, s32[128,2]{0,1:T(2,128)}, u32[]{:S(2)}) copy-start(s32[128,2]{0,1:T(2,128)} %param.14) | copy-start | bytes 3076
  6.9 0.9 %copy-start = (f32[128,2,128]{2,1,0:T(2,128)S(1)}, f32[128,2,128]{2,1,0:T(2,128)}, u32[]{:S(2)}) copy-start(f32[128,2,128]{2,1,0:T(2,128)} %param.10) | copy-start | bytes 393220
  6.9 1.0 %copy-start.1 = (f32[2,128,128]{2,1,0:T(8,128)S(1)}, f32[2,128,128]{2,1,0:T(8,128)}, u32[]{:S(2)}) copy-start(f32[2,128,128]{2,1,0:T(8,128)} %rad_ref.1) | copy-start | bytes 393220
